TPU v7x, 32 devices: a whole 2x2x4 slice. The times are simulated.
32 devices in a mesh: pipe: 2 (over x), row: 8 (over z, core), col: 2 (over y).
Axes of the slice: x: 2, y: 2, z: 4, core: 2. Of those that a mesh axis runs over, the one named last changes fastest.
Arguments:
- inputs: bfloat16 [4, 8, 1024, 512], P(None, 'row', 'col'), may hold values from -6 to 6
- first_gain: float32 [2, 512], P('pipe'), may hold values from 0.5 to 1.5
- first_shift: float32 [2, 512], P('pipe'), may hold values from -1.75 to 1.75
- qkv_weight: bfloat16 [2, 3, 512, 512], P('pipe', None, 'row', 'col'), may hold values from -0.25 to 0.25
- query_bias: float32 [2, 512], P('pipe', 'col'), may hold values from -3 to 3
- value_bias: float32 [2, 512], P('pipe', 'col'), may hold values from -1.75 to 1.75
- proj_weight: bfloat16 [2, 512, 512], P('pipe', 'col', 'row'), may hold values from -1 to 1
- proj_bias: float32 [2, 512], P('pipe'), may hold values from -1.75 to 1.75
- second_gain: float32 [2, 512], P('pipe'), may hold values from 0.5 to 1.5
- second_shift: float32 [2, 512], P('pipe'), may hold values from -1.75 to 1.75
- up_weight: bfloat16 [2, 512, 2048], P('pipe', 'row', 'col'), may hold values from -0.25 to 0.25
- up_bias: float32 [2, 2048], P('pipe', 'col'), may hold values from -3 to 3
- down_weight: bfloat16 [2, 2048, 512], P('pipe', 'col', 'row'), may hold values from -0.125 to 0.125
- down_bias: float32 [2, 512], P('pipe'), may hold values from -1.75 to 1.75
- cotangent: bfloat16 [4, 8, 1024, 512], P(None, 'row', 'col'), may hold values from -6 to 6
- live_clips: int32 [4, 8], P(None, 'row'), may hold values 0 or 1
Outputs:
- states: bfloat16 [2, 4, 8, 1024, 512], P('pipe', None, 'row', 'col')
- state_grads: float32 [2, 4, 8, 1024, 512], P('pipe', None, 'row', 'col')
- grad_first_gain: float32 [2, 512], P('pipe')
- grad_first_shift: float32 [2, 512], P('pipe')
- grad_qkv_weight: float32 [2, 3, 512, 512], P('pipe', None, 'row', 'col')
- grad_query_bias: float32 [2, 512], P('pipe', 'col')
- grad_value_bias: float32 [2, 512], P('pipe', 'col')
- grad_proj_weight: float32 [2, 512, 512], P('pipe', 'col', 'row')
- grad_proj_bias: float32 [2, 512], P('pipe')
- grad_second_gain: float32 [2, 512], P('pipe')
- grad_second_shift: float32 [2, 512], P('pipe')
- grad_up_weight: float32 [2, 512, 2048], P('pipe', 'row', 'col')
- grad_up_bias: float32 [2, 2048], P('pipe', 'col')
- grad_down_weight: float32 [2, 2048, 512], P('pipe', 'col', 'row')
- grad_down_bias: float32 [2, 512], P('pipe')
All inputs are finite; a program needn't handle non-finite values. No bound on the sum of `live_clips` on one device may be relied on, other than what follows from the above.
Results may differ from a plain program's by a relative error of at most 0.015.
Values may be sent and summed in bfloat16 or wider, within the bound.
A program may use at most 192 MiB of HBM per device.

v0:
```python
import math

import jax
import jax.numpy as jnp
from jax import lax
from jax.sharding import PartitionSpec as P

HD = 64


epsilon = 1e-05


def from_behind(value, axis, steps):
    count = lax.axis_size(axis)
    first, last = (max(0, -steps), min(count, count - steps))
    return lax.ppermute(value, axis, [(source, source + steps) for source in range(first, last)])


def exact_gelu(values):
    return jax.nn.gelu(values, approximate=False)


def spread_features(normed):
    return lax.all_gather(normed, "col", axis=0, tiled=True)


def sum_columns(partial_rows):
    return lax.psum_scatter(partial_rows, "col", scatter_dimension=0, tiled=True)


def spread_grads(grad_low):
    return lax.all_gather(grad_low, "col", axis=0, tiled=True)


def sum_grad_columns(partial_rows):
    return lax.psum_scatter(partial_rows, "col", scatter_dimension=0, tiled=True)


def norm_forward(values, gain, shift):
    row_mean = jnp.mean(values, axis=-1, keepdims=True)
    row_var = jnp.mean(jnp.square(values - row_mean), axis=-1, keepdims=True)
    inv_std = lax.rsqrt(row_var + epsilon)
    centered = (values - row_mean) * inv_std
    return (centered, inv_std[:, 0], (centered * gain + shift).astype(jnp.bfloat16))


def norm_backward(grad_norm, centered, inv_std, gain):
    grad_gain = jnp.sum(grad_norm * centered, axis=0)
    grad_shift = jnp.sum(grad_norm, axis=0)
    scaled = grad_norm * gain
    first = jnp.mean(scaled, axis=-1, keepdims=True)
    second = jnp.mean(scaled * centered, axis=-1, keepdims=True)
    grad_in = inv_std[:, None] * (scaled - first - centered * second)
    return (grad_in, grad_gain, grad_shift)


def attention_probs(query_heads, key_heads):
    score_scale = 1.0 / math.sqrt(HD)
    scores = (
        jnp.einsum("qhd,khd->hqk", query_heads, key_heads, preferred_element_type=jnp.float32)
        * score_scale
    )
    return jax.nn.softmax(scores, axis=-1)


def layer_forward(values, weights, params):
    qkv_full, proj_full, up_full, down_full = weights
    (
        gain_one,
        shift_one,
        query_bias,
        value_bias,
        proj_bias,
        gain_two,
        shift_two,
        up_bias,
        down_bias,
    ) = params
    head_count = qkv_full.shape[2] // HD
    centered_one, inv_one, normed_one = norm_forward(values, gain_one, shift_one)
    attn_input = spread_features(normed_one)
    frame_count = attn_input.shape[0]
    projected = jnp.einsum("sd,jde->jse", attn_input, qkv_full, preferred_element_type=jnp.float32)
    query_heads = (
        (projected[0] + query_bias).astype(jnp.bfloat16).reshape(frame_count, head_count, HD)
    )
    key_heads = projected[1].astype(jnp.bfloat16).reshape(frame_count, head_count, HD)
    value_heads = (
        (projected[2] + value_bias).astype(jnp.bfloat16).reshape(frame_count, head_count, HD)
    )
    softmax_out = attention_probs(query_heads, key_heads)
    context = jnp.einsum(
        "hqk,khd->qhd",
        softmax_out.astype(jnp.bfloat16),
        value_heads,
        preferred_element_type=jnp.float32,
    )
    context = context.reshape(frame_count, head_count * HD).astype(jnp.bfloat16)
    attended = (
        sum_columns(jnp.dot(context, proj_full, preferred_element_type=jnp.float32)) + proj_bias
    )
    hidden = values + attended
    centered_two, inv_two, normed_two = norm_forward(hidden, gain_two, shift_two)
    mlp_input = spread_features(normed_two)
    pre_act = jnp.dot(mlp_input, up_full, preferred_element_type=jnp.float32) + up_bias
    activated = exact_gelu(pre_act).astype(jnp.bfloat16)
    output = (
        hidden
        + sum_columns(jnp.dot(activated, down_full, preferred_element_type=jnp.float32))
        + down_bias
    )
    kept = (
        centered_one,
        inv_one,
        attn_input,
        query_heads,
        key_heads,
        value_heads,
        context,
        centered_two,
        inv_two,
        mlp_input,
        pre_act,
        activated,
    )
    return (output, kept)


def layer_backward(grad_out, kept, weights, params):
    qkv_full, proj_full, up_full, down_full = weights
    (
        gain_one,
        shift_one,
        query_bias,
        value_bias,
        proj_bias,
        gain_two,
        shift_two,
        up_bias,
        down_bias,
    ) = params
    (
        centered_one,
        inv_one,
        attn_input,
        query_heads,
        key_heads,
        value_heads,
        context,
        centered_two,
        inv_two,
        mlp_input,
        pre_act,
        activated,
    ) = kept
    frame_count = attn_input.shape[0]
    score_scale = 1.0 / math.sqrt(HD)
    grad_down_bias = jnp.sum(grad_out, axis=0)
    down_grad = spread_grads(grad_out.astype(jnp.bfloat16))
    grad_down = jnp.einsum("sf,sd->fd", activated, down_grad, preferred_element_type=jnp.float32)
    grad_act = jnp.einsum("sd,fd->sf", down_grad, down_full, preferred_element_type=jnp.float32)
    unused, gelu_pull = jax.vjp(exact_gelu, pre_act)
    grad_pre = gelu_pull(grad_act)[0]
    grad_up_bias = jnp.sum(grad_pre, axis=0)
    grad_pre_low = grad_pre.astype(jnp.bfloat16)
    grad_up = jnp.einsum("sd,sf->df", mlp_input, grad_pre_low, preferred_element_type=jnp.float32)
    grad_normed_two = sum_grad_columns(
        jnp.einsum("sf,df->sd", grad_pre_low, up_full, preferred_element_type=jnp.float32)
    )
    grad_hidden_norm, grad_gain_two, grad_shift_two = norm_backward(
        grad_normed_two, centered_two, inv_two, gain_two
    )
    grad_hidden = grad_out + grad_hidden_norm
    grad_proj_bias = jnp.sum(grad_hidden, axis=0)
    proj_grad = spread_grads(grad_hidden.astype(jnp.bfloat16))
    grad_proj = jnp.einsum("se,sd->ed", context, proj_grad, preferred_element_type=jnp.float32)
    grad_context = jnp.einsum("sd,ed->se", proj_grad, proj_full, preferred_element_type=jnp.float32)
    grad_context = grad_context.astype(jnp.bfloat16).reshape(query_heads.shape)
    softmax_out = attention_probs(query_heads, key_heads)
    grad_probs = jnp.einsum(
        "qhd,khd->hqk", grad_context, value_heads, preferred_element_type=jnp.float32
    )
    grad_value = jnp.einsum(
        "hqk,qhd->khd",
        softmax_out.astype(jnp.bfloat16),
        grad_context,
        preferred_element_type=jnp.float32,
    )
    grad_scores = softmax_out * (
        grad_probs - jnp.sum(softmax_out * grad_probs, axis=-1, keepdims=True)
    )
    scores_low = grad_scores.astype(jnp.bfloat16)
    grad_query = (
        jnp.einsum("hqk,khd->qhd", scores_low, key_heads, preferred_element_type=jnp.float32)
        * score_scale
    )
    grad_key = (
        jnp.einsum("hqk,qhd->khd", scores_low, query_heads, preferred_element_type=jnp.float32)
        * score_scale
    )
    grad_query = grad_query.reshape(frame_count, -1)
    grad_key = grad_key.reshape(frame_count, -1)
    grad_value = grad_value.reshape(frame_count, -1)
    grad_query_bias = jnp.sum(grad_query, axis=0)
    grad_value_bias = jnp.sum(grad_value, axis=0)
    grad_qkv_low = jnp.stack([grad_query, grad_key, grad_value]).astype(jnp.bfloat16)
    grad_qkv = jnp.einsum(
        "sd,jse->jde", attn_input, grad_qkv_low, preferred_element_type=jnp.float32
    )
    grad_normed_one = sum_grad_columns(
        jnp.einsum("jse,jde->sd", grad_qkv_low, qkv_full, preferred_element_type=jnp.float32)
    )
    grad_in_norm, grad_gain_one, grad_shift_one = norm_backward(
        grad_normed_one, centered_one, inv_one, gain_one
    )
    grad_in = grad_hidden + grad_in_norm
    weight_grads = (grad_qkv, grad_proj, grad_up, grad_down)
    vector_grads = (
        grad_gain_one,
        grad_shift_one,
        grad_query_bias,
        grad_value_bias,
        grad_proj_bias,
        grad_gain_two,
        grad_shift_two,
        grad_up_bias,
        grad_down_bias,
    )
    return (grad_in, weight_grads, vector_grads)


def store_slot(buffer, slot_index, is_valid, value):
    current = lax.dynamic_index_in_dim(buffer, slot_index, 0, keepdims=False)
    return lax.dynamic_update_index_in_dim(
        buffer, jnp.where(is_valid, value, current), slot_index, 0
    )


def reduce_end(weight_acc):
    return (
        lax.psum_scatter(
            weight_acc[0].astype(jnp.bfloat16), "row", scatter_dimension=1, tiled=True
        ).astype(jnp.float32),
        lax.psum_scatter(
            weight_acc[1].astype(jnp.bfloat16), "row", scatter_dimension=1, tiled=True
        ).astype(jnp.float32),
        lax.psum_scatter(
            weight_acc[2].astype(jnp.bfloat16), "row", scatter_dimension=0, tiled=True
        ).astype(jnp.float32),
        lax.psum_scatter(
            weight_acc[3].astype(jnp.bfloat16), "row", scatter_dimension=1, tiled=True
        ).astype(jnp.float32),
    )


def on_device(
    inputs,
    first_gain,
    first_shift,
    qkv_weight,
    query_bias,
    value_bias,
    proj_weight,
    proj_bias,
    second_gain,
    second_shift,
    up_weight,
    up_bias,
    down_weight,
    down_bias,
    cotangent,
    live_clips,
):
    micro_count = inputs.shape[0]
    row_count = inputs.shape[2]
    feature_count = inputs.shape[3]
    section_index = lax.axis_index("pipe")
    weights = (
        lax.all_gather(qkv_weight[0], "row", axis=1, tiled=True),
        lax.all_gather(proj_weight[0], "row", axis=1, tiled=True),
        lax.all_gather(up_weight[0], "row", axis=0, tiled=True),
        lax.all_gather(down_weight[0], "row", axis=1, tiled=True),
    )
    params = (
        first_gain[0],
        first_shift[0],
        query_bias[0],
        value_bias[0],
        proj_bias[0],
        second_gain[0],
        second_shift[0],
        up_bias[0],
        down_bias[0],
    )
    kept_buffers = ()
    zero_rows = jnp.zeros((row_count, feature_count), jnp.bfloat16)
    zero_stack = jnp.zeros((micro_count, row_count, feature_count), jnp.bfloat16)
    own_inputs = inputs[:, 0]

    def forward_tick(state_carry, tick_index):
        received, outputs, layer_inputs, buffers = state_carry
        batch_index = tick_index - section_index
        is_valid = (batch_index >= 0) & (batch_index < micro_count)
        slot_index = jnp.clip(batch_index, 0, micro_count - 1)
        own_input = lax.dynamic_index_in_dim(
            own_inputs, jnp.minimum(tick_index, micro_count - 1), 0, keepdims=False
        )
        layer_input = jnp.where(section_index == 0, own_input, received)
        output, kept = layer_forward(layer_input.astype(jnp.float32), weights, params)
        output_low = output.astype(jnp.bfloat16)
        passed = from_behind(output_low, "pipe", 1)
        outputs = store_slot(outputs, slot_index, is_valid, output_low)
        layer_inputs = store_slot(layer_inputs, slot_index, is_valid, layer_input)
        return ((passed, outputs, layer_inputs, buffers), None)

    tick_range = jnp.arange(micro_count + 1)
    forward_out, unused = lax.scan(
        forward_tick, (zero_rows, zero_stack, zero_stack, kept_buffers), tick_range
    )
    unused_rows, outputs, layer_inputs, kept_buffers = forward_out
    weight_acc = tuple((jnp.zeros(part.shape, jnp.float32) for part in weights))
    vector_acc = tuple((jnp.zeros(part.shape, jnp.float32) for part in params))
    grads_init = jnp.zeros((micro_count, row_count, feature_count), jnp.float32)
    live_rows = live_clips[:, 0]
    cot_rows_all = cotangent[:, 0]

    def backward_tick(state_carry, tick_index):
        received, grads_in, weight_sum, vector_sum = state_carry
        batch_index = micro_count - tick_index - section_index
        is_valid = (batch_index >= 0) & (batch_index < micro_count)
        slot_index = jnp.clip(batch_index, 0, micro_count - 1)
        cot_rows = lax.dynamic_index_in_dim(cot_rows_all, slot_index, 0, keepdims=False).astype(
            jnp.float32
        )
        live_flag = lax.dynamic_index_in_dim(live_rows, slot_index, 0, keepdims=False).astype(
            jnp.float32
        )
        grad_out = jnp.where(
            section_index == 1, cot_rows * live_flag, received.astype(jnp.float32)
        ) * is_valid.astype(jnp.float32)
        stored_input = lax.dynamic_index_in_dim(layer_inputs, slot_index, 0, keepdims=False)
        kept = layer_forward(stored_input.astype(jnp.float32), weights, params)[1]
        grad_in, weight_grads, vector_grads = layer_backward(grad_out, kept, weights, params)
        passed = from_behind(grad_in.astype(jnp.bfloat16), "pipe", -1)
        grads_in = store_slot(grads_in, slot_index, is_valid, grad_in)
        weight_sum = jax.tree.map(jnp.add, weight_sum, weight_grads)
        vector_sum = jax.tree.map(jnp.add, vector_sum, vector_grads)
        return ((passed, grads_in, weight_sum, vector_sum), None)

    backward_out, unused_two = lax.scan(
        backward_tick, (zero_rows, grads_init, weight_acc, vector_acc), tick_range
    )
    unused_grad, grads_in, weight_acc, vector_acc = backward_out
    weight_out = reduce_end(weight_acc)
    split_out = lax.psum((vector_acc[2], vector_acc[3], vector_acc[7]), "row")
    whole_out = lax.psum(
        (vector_acc[0], vector_acc[1], vector_acc[4], vector_acc[5], vector_acc[6], vector_acc[8]),
        ("row", "col"),
    )
    return (
        outputs[None, :, None],
        grads_in[None, :, None],
        whole_out[0][None],
        whole_out[1][None],
        weight_out[0][None],
        split_out[0][None],
        split_out[1][None],
        weight_out[1][None],
        whole_out[2][None],
        whole_out[3][None],
        whole_out[4][None],
        weight_out[2][None],
        split_out[2][None],
        weight_out[3][None],
        whole_out[5][None],
    )


def solution(mesh):
    placed = (
        P(None, "row", "col", None),
        P("pipe", None),
        P("pipe", None),
        P("pipe", None, "row", "col"),
        P("pipe", "col"),
        P("pipe", "col"),
        P("pipe", "col", "row"),
        P("pipe", None),
        P("pipe", None),
        P("pipe", None),
        P("pipe", "row", "col"),
        P("pipe", "col"),
        P("pipe", "col", "row"),
        P("pipe", None),
        P(None, "row", "col", None),
        P(None, "row"),
    )
    return jax.shard_map(
        on_device,
        mesh=mesh,
        in_specs=placed,
        out_specs=(
            P("pipe", None, "row", "col", None),
            P("pipe", None, "row", "col", None),
            P("pipe", None),
            P("pipe", None),
            P("pipe", None, "row", "col"),
            P("pipe", "col"),
            P("pipe", "col"),
            P("pipe", "col", "row"),
            P("pipe", None),
            P("pipe", None),
            P("pipe", None),
            P("pipe", "row", "col"),
            P("pipe", "col"),
            P("pipe", "col", "row"),
            P("pipe", None),
        ),
        check_vma=False,
    )
```

profile of v0, /device:TPU:0, one launch (start us, length us, event | category | flops | bytes accessed | tf_op | source)
XLA Modules:
  0.0 2830.5 jit_solution(8740462381904181484)
XLA Ops:
  25.8 18.5 all-gather
  61.8 961.5 %while.55 = (s32[]{:T(128)}, bf16[512,512]{1,0:T(8,128)(2,1)S(1)}, bf16[4,512,512]{2,1,0:T(8,128)(2,1)}, bf16[4,512,512]{2,1,0:T(8,128)(2,1)}, pred[]{:T(512)}, ...) while((s32[]{:T(128)}, bf16[512,512]{1,0:T(8,128)(2,1)S(1)}, ...), condition=%wide.region_9.10_spmd, body=%wide.region_0.9_spmd.sunk | while | flops 4413463552 | bytes 122786912 | solution.py:318
  70.8 19.0 all-gather.17.cloned.1.call-done
  131.7 31.9 %reduce-scatter.18.cloned.1.call-done = f32[512,512]{1,0:T(8,128)} async-done(((f32[1024,512]{1,0:T(8,128)}), f32[512,512]{1,0:T(8,128)}) %reduce-scatter.18.cloned.1.call-update) | async-done | bytes 1048592 | tf_op jit(solution)/shard_map/while/body/eval_jaxpr/reduce_scatter | solution.py:29
  169.0 21.4 all-gather.19.cloned.1.call-done
  205.1 30.9 %reduce-scatter.20.cloned.1.call-done = f32[512,512]{1,0:T(8,128)} async-done(((f32[1024,512]{1,0:T(8,128)}), f32[512,512]{1,0:T(8,128)}) %reduce-scatter.20.cloned.1.call-update) | async-done | bytes 1048592 | tf_op jit(solution)/shard_map/while/body/eval_jaxpr/reduce_scatter | solution.py:29
  262.0 20.3 all-gather.17.cloned.1.call-done
  324.3 31.9 %reduce-scatter.18.cloned.1.call-done = f32[512,512]{1,0:T(8,128)} async-done(((f32[1024,512]{1,0:T(8,128)}), f32[512,512]{1,0:T(8,128)}) %reduce-scatter.18.cloned.1.call-update) | async-done | bytes 1048592 | tf_op jit(solution)/shard_map/while/body/eval_jaxpr/reduce_scatter | solution.py:29
  361.6 21.4 all-gather.19.cloned.1.call-done
  397.6 30.9 %reduce-scatter.20.cloned.1.call-done = f32[512,512]{1,0:T(8,128)} async-done(((f32[1024,512]{1,0:T(8,128)}), f32[512,512]{1,0:T(8,128)}) %reduce-scatter.20.cloned.1.call-update) | async-done | bytes 1048592 | tf_op jit(solution)/shard_map/while/body/eval_jaxpr/reduce_scatter | solution.py:29
  454.5 20.3 all-gather.17.cloned.1.call-done
  516.7 31.9 %reduce-scatter.18.cloned.1.call-done = f32[512,512]{1,0:T(8,128)} async-done(((f32[1024,512]{1,0:T(8,128)}), f32[512,512]{1,0:T(8,128)}) %reduce-scatter.18.cloned.1.call-update) | async-done | bytes 1048592 | tf_op jit(solution)/shard_map/while/body/eval_jaxpr/reduce_scatter | solution.py:29
  554.0 21.4 all-gather.19.cloned.1.call-done
  590.1 30.9 %reduce-scatter.20.cloned.1.call-done = f32[512,512]{1,0:T(8,128)} async-done(((f32[1024,512]{1,0:T(8,128)}), f32[512,512]{1,0:T(8,128)}) %reduce-scatter.20.cloned.1.call-update) | async-done | bytes 1048592 | tf_op jit(solution)/shard_map/while/body/eval_jaxpr/reduce_scatter | solution.py:29
  647.0 20.3 all-gather.17.cloned.1.call-done
  709.2 31.9 %reduce-scatter.18.cloned.1.call-done = f32[512,512]{1,0:T(8,128)} async-done(((f32[1024,512]{1,0:T(8,128)}), f32[512,512]{1,0:T(8,128)}) %reduce-scatter.18.cloned.1.call-update) | async-done | bytes 1048592 | tf_op jit(solution)/shard_map/while/body/eval_jaxpr/reduce_scatter | solution.py:29
  746.5 21.4 all-gather.19.cloned.1.call-done
  782.6 30.9 %reduce-scatter.20.cloned.1.call-done = f32[512,512]{1,0:T(8,128)} async-done(((f32[1024,512]{1,0:T(8,128)}), f32[512,512]{1,0:T(8,128)}) %reduce-scatter.20.cloned.1.call-update) | async-done | bytes 1048592 | tf_op jit(solution)/shard_map/while/body/eval_jaxpr/reduce_scatter | solution.py:29
  839.5 20.3 all-gather.17.cloned.1.call-done
  901.7 31.9 %reduce-scatter.18.cloned.1.call-done = f32[512,512]{1,0:T(8,128)} async-done(((f32[1024,512]{1,0:T(8,128)}), f32[512,512]{1,0:T(8,128)}) %reduce-scatter.18.cloned.1.call-update) | async-done | bytes 1048592 | tf_op jit(solution)/shard_map/while/body/eval_jaxpr/reduce_scatter | solution.py:29
  939.0 21.4 all-gather.19.cloned.1.call-done
  975.1 30.9 %reduce-scatter.20.cloned.1.call-done = f32[512,512]{1,0:T(8,128)} async-done(((f32[1024,512]{1,0:T(8,128)}), f32[512,512]{1,0:T(8,128)}) %reduce-scatter.20.cloned.1.call-update) | async-done | bytes 1048592 | tf_op jit(solution)/shard_map/while/body/eval_jaxpr/reduce_scatter | solution.py:29
  1027.3 1663.7 %while.56 = (s32[]{:T(128)}, bf16[512,512]{1,0:T(8,128)(2,1)}, f32[4,512,512]{2,1,0:T(8,128)}, f32[3,512,256]{1,2,0:T(8,128)}, f32[256,512]{1,0:T(8,128)}, /*ind...) while((s32[]{:T(128)}, bf16[512,512]{1,0:T(8,128)(2,1)}, ...), condition=%wide.region_34.35_spmd.clone, body=%wide.region_10.34_spmd.clone.sunk | while | flops 12016956416 | bytes 501957632 | solution.py:351
  1059.1 20.3 all-gather.21.cloned.1.call-done
  1091.0 19.1 fusion.289
  1129.0 31.9 %reduce-scatter.22.cloned.1.call-done = f32[512,512]{1,0:T(8,128)} async-done(((f32[1024,512]{1,0:T(8,128)}), f32[512,512]{1,0:T(8,128)}) %reduce-scatter.22.cloned.1.call-update) | async-done | bytes 1048592 | tf_op jit(solution)/shard_map/while/body/eval_jaxpr/reduce_scatter | solution.py:29
  1218.2 31.9 %reduce-scatter.24.cloned.1.call-done = f32[512,512]{1,0:T(8,128)} async-done(((f32[1024,512]{1,0:T(8,128)}), f32[512,512]{1,0:T(8,128)}) %reduce-scatter.24.cloned.1.call-update) | async-done | bytes 1048592 | tf_op jit(solution)/shard_map/while/body/eval_jaxpr/reduce_scatter | solution.py:37
  1256.2 21.4 all-gather.27.cloned.1.call-done
  1418.8 19.1 fusion.289
  1456.8 31.9 %reduce-scatter.22.cloned.1.call-done = f32[512,512]{1,0:T(8,128)} async-done(((f32[1024,512]{1,0:T(8,128)}), f32[512,512]{1,0:T(8,128)}) %reduce-scatter.22.cloned.1.call-update) | async-done | bytes 1048592 | tf_op jit(solution)/shard_map/while/body/eval_jaxpr/reduce_scatter | solution.py:29
  1546.0 31.9 %reduce-scatter.24.cloned.1.call-done = f32[512,512]{1,0:T(8,128)} async-done(((f32[1024,512]{1,0:T(8,128)}), f32[512,512]{1,0:T(8,128)}) %reduce-scatter.24.cloned.1.call-update) | async-done | bytes 1048592 | tf_op jit(solution)/shard_map/while/body/eval_jaxpr/reduce_scatter | solution.py:37
  1584.0 21.4 all-gather.27.cloned.1.call-done
  1716.5 18.5 all-gather.21.cloned.1.call-done
  1746.6 19.1 fusion.289
  1784.6 31.9 %reduce-scatter.22.cloned.1.call-done = f32[512,512]{1,0:T(8,128)} async-done(((f32[1024,512]{1,0:T(8,128)}), f32[512,512]{1,0:T(8,128)}) %reduce-scatter.22.cloned.1.call-update) | async-done | bytes 1048592 | tf_op jit(solution)/shard_map/while/body/eval_jaxpr/reduce_scatter | solution.py:29
  1874.0 31.9 %reduce-scatter.24.cloned.1.call-done = f32[512,512]{1,0:T(8,128)} async-done(((f32[1024,512]{1,0:T(8,128)}), f32[512,512]{1,0:T(8,128)}) %reduce-scatter.24.cloned.1.call-update) | async-done | bytes 1048592 | tf_op jit(solution)/shard_map/while/body/eval_jaxpr/reduce_scatter | solution.py:37
  1911.9 21.4 all-gather.27.cloned.1.call-done
  2044.5 18.5 all-gather.21.cloned.1.call-done
  2074.5 19.1 fusion.289
  2112.5 31.9 %reduce-scatter.22.cloned.1.call-done = f32[512,512]{1,0:T(8,128)} async-done(((f32[1024,512]{1,0:T(8,128)}), f32[512,512]{1,0:T(8,128)}) %reduce-scatter.22.cloned.1.call-update) | async-done | bytes 1048592 | tf_op jit(solution)/shard_map/while/body/eval_jaxpr/reduce_scatter | solution.py:29
  2201.8 31.9 %reduce-scatter.24.cloned.1.call-done = f32[512,512]{1,0:T(8,128)} async-done(((f32[1024,512]{1,0:T(8,128)}), f32[512,512]{1,0:T(8,128)}) %reduce-scatter.24.cloned.1.call-update) | async-done | bytes 1048592 | tf_op jit(solution)/shard_map/while/body/eval_jaxpr/reduce_scatter | solution.py:37
  2239.7 21.4 all-gather.27.cloned.1.call-done
  2402.4 19.1 fusion.289
  2440.3 31.9 %reduce-scatter.22.cloned.1.call-done = f32[512,512]{1,0:T(8,128)} async-done(((f32[1024,512]{1,0:T(8,128)}), f32[512,512]{1,0:T(8,128)}) %reduce-scatter.22.cloned.1.call-update) | async-done | bytes 1048592 | tf_op jit(solution)/shard_map/while/body/eval_jaxpr/reduce_scatter | solution.py:29
  2529.8 31.9 %reduce-scatter.24.cloned.1.call-done = f32[512,512]{1,0:T(8,128)} async-done(((f32[1024,512]{1,0:T(8,128)}), f32[512,512]{1,0:T(8,128)}) %reduce-scatter.24.cloned.1.call-update) | async-done | bytes 1048592 | tf_op jit(solution)/shard_map/while/body/eval_jaxpr/reduce_scatter | solution.py:37
  2567.7 21.4 all-gather.27.cloned.1.call-done
  2716.6 58.3 %all-reduce = (f32[1,512]{1,0:T(1,128)}, f32[1,512]{1,0:T(1,128)}, f32[1,512]{1,0:T(1,128)}, f32[1,512]{1,0:T(1,128)}, f32[1,512]{1,0:T(1,128)}, /*index=5*/f32[1,512]{1,0:T(1,128)}) all-reduce(f32[1,512]{1,0:T(1,128)S(1)} %bitcast.384, f32[1,512]{1,0:T(1,128)S(1)} %bitcast.383, ...), channel_id=1, replica_groups=mesh['pipe'=2,'row'=8,'col'=2] {'row','col'}, use_global_device_ids=true, to_apply=%region_35.36 | all-reduce | flops 3072 | bytes 24576 | tf_op jit(solution)/shard_map/psum | solution.py:357
  2790.4 31.3 %reduce-scatter.16.cloned.1.call-done = bf16[1024,64]{0,1:T(8,128)(2,1)} async-done(((bf16[1024,512]{0,1:T(8,128)(2,1)}), bf16[1024,64]{0,1:T(8,128)(2,1)}) %reduce-scatter.16.cloned.1.call-update) | async-done | bytes 131088 | tf_op jit(solution)/shard_map/reduce_scatter | solution.py:251
  (1379 shorter events, 1564.7 us)
Async XLA Ops:
  7.9 50.9 %all-gather.13.cloned.1.call-start = ((), (), s32[]{:S(2)}) async-start(), calls=%async_computation.13 | async-start | bytes 1179648 | tf_op jit(solution)/shard_map/all_gather | solution.py:282
  68.8 94.9 %reduce-scatter.18.cloned.1.call-start = ((), (), s32[]{:S(2)}) async-start(), calls=%async_computation.16 | async-start | bytes 3145728 | tf_op jit(solution)/shard_map/while/body/eval_jaxpr/reduce_scatter | solution.py:29
  131.7 58.8 %all-gather.19.cloned.1.call-start = ((), (), s32[]{:S(2)}) async-start(), calls=%async_computation.17 | async-start | bytes 1572864 | tf_op jit(solution)/shard_map/while/body/eval_jaxpr/all_gather | solution.py:25
  169.0 67.0 %reduce-scatter.20.cloned.1.call-start = ((), (), s32[]{:S(2)}) async-start(), calls=%async_computation.18 | async-start | bytes 3145728 | tf_op jit(solution)/shard_map/while/body/eval_jaxpr/reduce_scatter | solution.py:29
  260.0 96.2 %reduce-scatter.18.cloned.1.call-start = ((), (), s32[]{:S(2)}) async-start(), calls=%async_computation.16 | async-start | bytes 3145728 | tf_op jit(solution)/shard_map/while/body/eval_jaxpr/reduce_scatter | solution.py:29
  324.2 58.8 %all-gather.19.cloned.1.call-start = ((), (), s32[]{:S(2)}) async-start(), calls=%async_computation.17 | async-start | bytes 1572864 | tf_op jit(solution)/shard_map/while/body/eval_jaxpr/all_gather | solution.py:25
  361.5 67.0 %reduce-scatter.20.cloned.1.call-start = ((), (), s32[]{:S(2)}) async-start(), calls=%async_computation.18 | async-start | bytes 3145728 | tf_op jit(solution)/shard_map/while/body/eval_jaxpr/reduce_scatter | solution.py:29
  452.5 96.2 %reduce-scatter.18.cloned.1.call-start = ((), (), s32[]{:S(2)}) async-start(), calls=%async_computation.16 | async-start | bytes 3145728 | tf_op jit(solution)/shard_map/while/body/eval_jaxpr/reduce_scatter | solution.py:29
  516.7 58.8 %all-gather.19.cloned.1.call-start = ((), (), s32[]{:S(2)}) async-start(), calls=%async_computation.17 | async-start | bytes 1572864 | tf_op jit(solution)/shard_map/while/body/eval_jaxpr/all_gather | solution.py:25
  554.0 67.0 %reduce-scatter.20.cloned.1.call-start = ((), (), s32[]{:S(2)}) async-start(), calls=%async_computation.18 | async-start | bytes 3145728 | tf_op jit(solution)/shard_map/while/body/eval_jaxpr/reduce_scatter | solution.py:29
  645.0 96.2 %reduce-scatter.18.cloned.1.call-start = ((), (), s32[]{:S(2)}) async-start(), calls=%async_computation.16 | async-start | bytes 3145728 | tf_op jit(solution)/shard_map/while/body/eval_jaxpr/reduce_scatter | solution.py:29
  709.2 58.8 %all-gather.19.cloned.1.call-start = ((), (), s32[]{:S(2)}) async-start(), calls=%async_computation.17 | async-start | bytes 1572864 | tf_op jit(solution)/shard_map/while/body/eval_jaxpr/all_gather | solution.py:25
  746.5 67.0 %reduce-scatter.20.cloned.1.call-start = ((), (), s32[]{:S(2)}) async-start(), calls=%async_computation.18 | async-start | bytes 3145728 | tf_op jit(solution)/shard_map/while/body/eval_jaxpr/reduce_scatter | solution.py:29
  837.5 96.2 %reduce-scatter.18.cloned.1.call-start = ((), (), s32[]{:S(2)}) async-start(), calls=%async_computation.16 | async-start | bytes 3145728 | tf_op jit(solution)/shard_map/while/body/eval_jaxpr/reduce_scatter | solution.py:29
  901.7 58.8 %all-gather.19.cloned.1.call-start = ((), (), s32[]{:S(2)}) async-start(), calls=%async_computation.17 | async-start | bytes 1572864 | tf_op jit(solution)/shard_map/while/body/eval_jaxpr/all_gather | solution.py:25
  939.0 67.0 %reduce-scatter.20.cloned.1.call-start = ((), (), s32[]{:S(2)}) async-start(), calls=%async_computation.18 | async-start | bytes 3145728 | tf_op jit(solution)/shard_map/while/body/eval_jaxpr/reduce_scatter | solution.py:29
  1057.0 103.8 %reduce-scatter.22.cloned.1.call-start = ((), (), s32[]{:S(2)}) async-start(), calls=%async_computation.20 | async-start | bytes 3145728 | tf_op jit(solution)/shard_map/while/body/eval_jaxpr/reduce_scatter | solution.py:29
  1128.9 56.3 %all-gather.23.cloned.1.call-start = ((), (), s32[]{:S(2)}) async-start(), calls=%async_computation.21 | async-start | bytes 1572864 | tf_op jit(solution)/shard_map/while/body/eval_jaxpr/all_gather | solution.py:25
  1163.8 44.3 %all-gather.25.cloned.1.call-start = ((), (), s32[]{:S(2)}) async-start(), calls=%async_computation.22 | async-start | bytes 1572864 | tf_op jit(solution)/shard_map/while/body/eval_jaxpr/all_gather | solution.py:33
  1168.0 82.2 %reduce-scatter.24.cloned.1.call-start = ((), (), s32[]{:S(2)}) async-start(), calls=%async_computation.23 | async-start | bytes 3145728 | tf_op jit(solution)/shard_map/while/body/eval_jaxpr/reduce_scatter | solution.py:37
  1218.2 59.4 %all-gather.27.cloned.1.call-start = ((), (), s32[]{:S(2)}) async-start(), calls=%async_computation.24 | async-start | bytes 1572864 | tf_op jit(solution)/shard_map/while/body/eval_jaxpr/all_gather | solution.py:33
  1256.1 102.7 %reduce-scatter.26.cloned.1.call-start = ((), (), s32[]{:S(2)}) async-start(), calls=%async_computation.25 | async-start | bytes 3145728 | tf_op jit(solution)/shard_map/while/body/eval_jaxpr/reduce_scatter | solution.py:37
  1386.7 102.0 %reduce-scatter.22.cloned.1.call-start = ((), (), s32[]{:S(2)}) async-start(), calls=%async_computation.20 | async-start | bytes 3145728 | tf_op jit(solution)/shard_map/while/body/eval_jaxpr/reduce_scatter | solution.py:29
  1456.7 56.3 %all-gather.23.cloned.1.call-start = ((), (), s32[]{:S(2)}) async-start(), calls=%async_computation.21 | async-start | bytes 1572864 | tf_op jit(solution)/shard_map/while/body/eval_jaxpr/all_gather | solution.py:25
  1495.8 82.2 %reduce-scatter.24.cloned.1.call-start = ((), (), s32[]{:S(2)}) async-start(), calls=%async_computation.23 | async-start | bytes 3145728 | tf_op jit(solution)/shard_map/while/body/eval_jaxpr/reduce_scatter | solution.py:37
  1546.0 59.4 %all-gather.27.cloned.1.call-start = ((), (), s32[]{:S(2)}) async-start(), calls=%async_computation.24 | async-start | bytes 1572864 | tf_op jit(solution)/shard_map/while/body/eval_jaxpr/all_gather | solution.py:33
  1583.9 102.7 %reduce-scatter.26.cloned.1.call-start = ((), (), s32[]{:S(2)}) async-start(), calls=%async_computation.25 | async-start | bytes 3145728 | tf_op jit(solution)/shard_map/while/body/eval_jaxpr/reduce_scatter | solution.py:37
  1714.5 102.0 %reduce-scatter.22.cloned.1.call-start = ((), (), s32[]{:S(2)}) async-start(), calls=%async_computation.20 | async-start | bytes 3145728 | tf_op jit(solution)/shard_map/while/body/eval_jaxpr/reduce_scatter | solution.py:29
  1784.5 56.3 %all-gather.23.cloned.1.call-start = ((), (), s32[]{:S(2)}) async-start(), calls=%async_computation.21 | async-start | bytes 1572864 | tf_op jit(solution)/shard_map/while/body/eval_jaxpr/all_gather | solution.py:25
  1819.4 44.4 %all-gather.25.cloned.1.call-start = ((), (), s32[]{:S(2)}) async-start(), calls=%async_computation.22 | async-start | bytes 1572864 | tf_op jit(solution)/shard_map/while/body/eval_jaxpr/all_gather | solution.py:33
  1823.6 82.3 %reduce-scatter.24.cloned.1.call-start = ((), (), s32[]{:S(2)}) async-start(), calls=%async_computation.23 | async-start | bytes 3145728 | tf_op jit(solution)/shard_map/while/body/eval_jaxpr/reduce_scatter | solution.py:37
  1873.9 59.4 %all-gather.27.cloned.1.call-start = ((), (), s32[]{:S(2)}) async-start(), calls=%async_computation.24 | async-start | bytes 1572864 | tf_op jit(solution)/shard_map/while/body/eval_jaxpr/all_gather | solution.py:33
  1911.9 102.7 %reduce-scatter.26.cloned.1.call-start = ((), (), s32[]{:S(2)}) async-start(), calls=%async_computation.25 | async-start | bytes 3145728 | tf_op jit(solution)/shard_map/while/body/eval_jaxpr/reduce_scatter | solution.py:37
  2042.4 102.0 %reduce-scatter.22.cloned.1.call-start = ((), (), s32[]{:S(2)}) async-start(), calls=%async_computation.20 | async-start | bytes 3145728 | tf_op jit(solution)/shard_map/while/body/eval_jaxpr/reduce_scatter | solution.py:29
  2112.5 56.3 %all-gather.23.cloned.1.call-start = ((), (), s32[]{:S(2)}) async-start(), calls=%async_computation.21 | async-start | bytes 1572864 | tf_op jit(solution)/shard_map/while/body/eval_jaxpr/all_gather | solution.py:25
  2151.5 82.2 %reduce-scatter.24.cloned.1.call-start = ((), (), s32[]{:S(2)}) async-start(), calls=%async_computation.23 | async-start | bytes 3145728 | tf_op jit(solution)/shard_map/while/body/eval_jaxpr/reduce_scatter | solution.py:37
  2201.7 59.4 %all-gather.27.cloned.1.call-start = ((), (), s32[]{:S(2)}) async-start(), calls=%async_computation.24 | async-start | bytes 1572864 | tf_op jit(solution)/shard_map/while/body/eval_jaxpr/all_gather | solution.py:33
  2239.7 102.7 %reduce-scatter.26.cloned.1.call-start = ((), (), s32[]{:S(2)}) async-start(), calls=%async_computation.25 | async-start | bytes 3145728 | tf_op jit(solution)/shard_map/while/body/eval_jaxpr/reduce_scatter | solution.py:37
  2370.3 102.0 %reduce-scatter.22.cloned.1.call-start = ((), (), s32[]{:S(2)}) async-start(), calls=%async_computation.20 | async-start | bytes 3145728 | tf_op jit(solution)/shard_map/while/body/eval_jaxpr/reduce_scatter | solution.py:29
  2440.3 56.3 %all-gather.23.cloned.1.call-start = ((), (), s32[]{:S(2)}) async-start(), calls=%async_computation.21 | async-start | bytes 1572864 | tf_op jit(solution)/shard_map/while/body/eval_jaxpr/all_gather | solution.py:25
  2475.2 44.4 %all-gather.25.cloned.1.call-start = ((), (), s32[]{:S(2)}) async-start(), calls=%async_computation.22 | async-start | bytes 1572864 | tf_op jit(solution)/shard_map/while/body/eval_jaxpr/all_gather | solution.py:33
  2479.3 82.3 %reduce-scatter.24.cloned.1.call-start = ((), (), s32[]{:S(2)}) async-start(), calls=%async_computation.23 | async-start | bytes 3145728 | tf_op jit(solution)/shard_map/while/body/eval_jaxpr/reduce_scatter | solution.py:37
  2529.7 59.4 %all-gather.27.cloned.1.call-start = ((), (), s32[]{:S(2)}) async-start(), calls=%async_computation.24 | async-start | bytes 1572864 | tf_op jit(solution)/shard_map/while/body/eval_jaxpr/all_gather | solution.py:33
  2567.6 102.7 %reduce-scatter.26.cloned.1.call-start = ((), (), s32[]{:S(2)}) async-start(), calls=%async_computation.25 | async-start | bytes 3145728 | tf_op jit(solution)/shard_map/while/body/eval_jaxpr/reduce_scatter | solution.py:37
  2691.0 83.9 %reduce-scatter.12.cloned.1.call-start = ((), (), s32[]{:S(2)}) async-start(), calls=%async_computation.10 | async-start | bytes 294912 | tf_op jit(solution)/shard_map/reduce_scatter | solution.py:245
  2693.1 83.2 %reduce-scatter.10.cloned.1.call-start = ((), (), s32[]{:S(2)}) async-start(), calls=%async_computation.9 | async-start | bytes 884736 | tf_op jit(solution)/shard_map/reduce_scatter | solution.py:242
  2695.7 93.1 %reduce-scatter.14.cloned.1.call-start = ((), (), s32[]{:S(2)}) async-start(), calls=%async_computation.11 | async-start | bytes 1179648 | tf_op jit(solution)/shard_map/reduce_scatter | solution.py:248
  2698.7 123.0 %reduce-scatter.16.cloned.1.call-start = ((), (), s32[]{:S(2)}) async-start(), calls=%async_computation.12 | async-start | bytes 1179648 | tf_op jit(solution)/shard_map/reduce_scatter | solution.py:251
  (399 other events, 6848.4 us)
Sparse Core Ops, SparseCore 0:
  9.6 26.7 all-gather.14
  131.8 31.8 reduce-scatter.17
  169.1 21.2 all-gather.18
  204.1 31.8 reduce-scatter.19
  260.1 22.2 all-gather.16
  324.3 31.8 reduce-scatter.17
  396.6 31.8 reduce-scatter.19
  452.6 22.2 all-gather.16
  516.8 31.8 reduce-scatter.17
  589.1 31.8 reduce-scatter.19
  645.1 22.2 all-gather.16
  709.3 31.8 reduce-scatter.17
  746.6 21.2 all-gather.18
  781.6 31.8 reduce-scatter.19
  837.6 22.2 all-gather.16
  901.8 31.8 reduce-scatter.17
  939.1 21.2 all-gather.18
  974.1 31.8 reduce-scatter.19
  1057.2 22.2 all-gather.20
  1129.0 31.8 reduce-scatter.21
  1163.9 21.2 all-gather.22
  1218.3 31.8 reduce-scatter.23
  1256.2 21.3 all-gather.26
  1326.9 31.8 reduce-scatter.25
  1456.8 31.8 reduce-scatter.21
  1491.7 21.2 all-gather.22
  1546.1 31.8 reduce-scatter.23
  1584.0 21.3 all-gather.26
  1654.7 31.8 reduce-scatter.25
  1784.6 31.8 reduce-scatter.21
  1819.5 21.2 all-gather.22
  1874.1 31.8 reduce-scatter.23
  1912.0 21.3 all-gather.26
  1982.7 31.8 reduce-scatter.25
  2112.6 31.8 reduce-scatter.21
  2147.5 21.2 all-gather.22
  2201.9 31.8 reduce-scatter.23
  2239.8 21.3 all-gather.26
  2310.5 31.8 reduce-scatter.25
  2440.4 31.8 reduce-scatter.21
  2475.3 21.2 all-gather.22
  2529.8 31.8 reduce-scatter.23
  2567.8 21.3 all-gather.26
  2638.4 31.8 reduce-scatter.25
  2694.3 29.5 reduce-scatter.11
  2726.1 29.6 reduce-scatter.9
  2758.1 30.6 reduce-scatter.13
  2791.1 30.5 reduce-scatter.15
  (13 shorter events, 271.7 us)
where the time goes:
time: 2840 us; the launch traced here: 2830 us
  waiting for transfers between devices  1450 us (51%)
  matrix products  729 us (26%)
  other arithmetic  380 us (13%)
  blocking collectives  109 us (4%)
  local copies, waits for them, and re-layouts  83.2 us (3%)
  loops' own time  42.2 us (1%)
    reduce_scatter x15, waiting for transfers between devices, sum_columns(): lax.psum_scatter(partial_rows, 'col', scatter_dimension=0, tiled=True)  474 us
    all_gather x20, waiting for transfers between devices, spread_features(): return lax.all_gather(normed, 'col', axis=0, tiled=True)  388 us
    reduce_scatter x10, waiting for transfers between devices, sum_grad_columns(): lax.psum_scatter(partial_rows, 'col', scatter_dimension=0, tiled=True)  246 us
    sub x10, other arithmetic, attention_probs(): return jax.nn.softmax(scores, axis=-1)  158 us
    all_gather x10, waiting for transfers between devices, spread_grads(): return lax.all_gather(grad_low, 'col', axis=0, tiled=True)  158 us
    dot_general x10, matrix products, layer_forward(): jnp.einsum('hqk,khd->qhd', softmax_out.astype(jnp.bfloat16), value_heads,...  158 us
    ppermute x10, waiting for transfers between devices, from_behind(): lax.ppermute(value, axis, [(source, source + steps) for source in range(f...  126 us
    dot_general x5, matrix products, layer_backward(): jnp.einsum('qhd,khd->hqk', grad_context, value_heads, preferred_element_t...  82.3 us
  transfers between devices with their start and end apart: 71, of which 68 were waited for; matrix products, arithmetic and copies ran while one was open for 7% of the time, Pallas kernels for 0%

commit v1 on v0

--- a/solution.py
+++ b/solution.py
@@ -3,6 +3,8 @@
 import jax
 import jax.numpy as jnp
 from jax import lax
+from jax.experimental import pallas as pl
+from jax.experimental.pallas import tpu as pltpu
 from jax.sharding import PartitionSpec as P
 
 HD = 64
@@ -377,6 +379,483 @@
     )
 
 
+def contract(left, right, left_dim, right_dim):
+    return lax.dot_general(
+        left, right, (((left_dim,), (right_dim,)), ((), ())), preferred_element_type=jnp.float32
+    )
+
+
+QUERY_BLOCK = 256
+
+
+def attention_forward_kernel(q_ref, k_ref, v_ref, context_ref, lse_ref):
+    frames = q_ref.shape[0]
+    score_scale = 1.0 / math.sqrt(HD)
+    for start in range(0, frames, QUERY_BLOCK):
+        rows = slice(start, start + QUERY_BLOCK)
+        parts = []
+        for head in range(2):
+            lanes = slice(head * HD, (head + 1) * HD)
+            scaled = q_ref[rows, lanes] * jnp.asarray(score_scale, jnp.bfloat16)
+            scores = contract(k_ref[:, lanes], scaled, 1, 1)
+            top = jnp.max(scores, axis=0, keepdims=True)
+            weights = jnp.exp(scores - top)
+            total = jnp.sum(weights, axis=0, keepdims=True)
+            mixed = contract(v_ref[:, lanes], weights.astype(jnp.bfloat16), 0, 0)
+            parts.append(mixed / total)
+            lse_ref[0, head : head + 1, rows] = top + jnp.log(total)
+        pair = jnp.concatenate(parts, axis=0)
+        context_ref[rows, :] = pair.T.astype(jnp.bfloat16)
+
+
+def attention_forward(qkv):
+    frames = qkv.shape[0]
+    width = qkv.shape[1] // 3
+    pairs = width // (2 * HD)
+
+    def column(part):
+        return pl.BlockSpec((frames, 2 * HD), lambda pair: (0, pair + part * pairs))
+
+    return pl.pallas_call(
+        attention_forward_kernel,
+        grid=(pairs,),
+        in_specs=[column(0), column(1), column(2)],
+        out_specs=[
+            pl.BlockSpec((frames, 2 * HD), lambda pair: (0, pair)),
+            pl.BlockSpec((1, 8, frames), lambda pair: (pair, 0, 0)),
+        ],
+        out_shape=[
+            jax.ShapeDtypeStruct((frames, width), jnp.bfloat16),
+            jax.ShapeDtypeStruct((pairs, 8, frames), jnp.float32),
+        ],
+        compiler_params=pltpu.CompilerParams(vmem_limit_bytes=40 * 1024 * 1024),
+        cost_estimate=pl.CostEstimate(
+            flops=4 * frames * frames * width,
+            bytes_accessed=8 * frames * width,
+            transcendentals=frames * frames * width // HD,
+        ),
+        name="attention_forward",
+    )(qkv, qkv, qkv)
+
+
+def attention_backward_kernel(q_ref, k_ref, v_ref, grad_ref, lse_ref, out_ref, bias_ref):
+    frames = q_ref.shape[0]
+    width = out_ref.shape[1] // 3
+    pair_index = pl.program_id(0)
+    score_scale = 1.0 / math.sqrt(HD)
+    grad_keys = [None, None]
+    grad_values = [None, None]
+    query_total = jnp.zeros((1, 2 * HD), jnp.float32)
+
+    def columns(part):
+        return pl.ds(pl.multiple_of(part * width + pair_index * (2 * HD), 2 * HD), 2 * HD)
+
+    for start in range(0, frames, QUERY_BLOCK):
+        rows = slice(start, start + QUERY_BLOCK)
+        parts = []
+        for head in range(2):
+            lanes = slice(head * HD, (head + 1) * HD)
+            keys = k_ref[:, lanes]
+            grads = grad_ref[rows, lanes]
+            scaled = q_ref[rows, lanes] * jnp.asarray(score_scale, jnp.bfloat16)
+            scores = contract(keys, scaled, 1, 1)
+            probs = jnp.exp(scores - lse_ref[0, head : head + 1, rows])
+            grad_probs = contract(v_ref[:, lanes], grads, 1, 1)
+            delta = jnp.sum(probs * grad_probs, axis=0, keepdims=True)
+            low_scores = (probs * (grad_probs - delta)).astype(jnp.bfloat16)
+            value_part = contract(probs.astype(jnp.bfloat16), grads, 1, 0)
+            key_part = contract(low_scores, scaled, 1, 0)
+            grad_values[head] = value_part if start == 0 else grad_values[head] + value_part
+            grad_keys[head] = key_part if start == 0 else grad_keys[head] + key_part
+            parts.append(contract(keys, low_scores, 0, 0))
+        pair = jnp.concatenate(parts, axis=0).T * score_scale
+        query_total = query_total + jnp.sum(pair, axis=0, keepdims=True)
+        out_ref[rows, columns(0)] = pair.astype(jnp.bfloat16)
+    key_pair = jnp.concatenate(grad_keys, axis=1)
+    value_pair = jnp.concatenate(grad_values, axis=1)
+    out_ref[:, columns(1)] = key_pair.astype(jnp.bfloat16)
+    out_ref[:, columns(2)] = value_pair.astype(jnp.bfloat16)
+    bias_ref[0:1, columns(0)] = query_total
+    bias_ref[0:1, columns(2)] = jnp.sum(value_pair, axis=0, keepdims=True)
+
+
+def attention_backward(qkv, grad_context, lse):
+    frames = qkv.shape[0]
+    width = qkv.shape[1] // 3
+    pairs = width // (2 * HD)
+
+    def column(part):
+        return pl.BlockSpec((frames, 2 * HD), lambda pair: (0, pair + part * pairs))
+
+    return pl.pallas_call(
+        attention_backward_kernel,
+        grid=(pairs,),
+        in_specs=[
+            column(0),
+            column(1),
+            column(2),
+            column(0),
+            pl.BlockSpec((1, 8, frames), lambda pair: (pair, 0, 0)),
+        ],
+        out_specs=[
+            pl.BlockSpec((frames, 3 * width), lambda pair: (0, 0)),
+            pl.BlockSpec((8, 3 * width), lambda pair: (0, 0)),
+        ],
+        out_shape=[
+            jax.ShapeDtypeStruct((frames, 3 * width), jnp.bfloat16),
+            jax.ShapeDtypeStruct((8, 3 * width), jnp.float32),
+        ],
+        compiler_params=pltpu.CompilerParams(vmem_limit_bytes=40 * 1024 * 1024),
+        cost_estimate=pl.CostEstimate(
+            flops=10 * frames * frames * width,
+            bytes_accessed=14 * frames * width,
+            transcendentals=frames * frames * width // HD,
+        ),
+        name="attention_backward",
+    )(qkv, qkv, qkv, grad_context, lse)
+
+
+def cut_block(block, width, hidden):
+    edge = 4 * width
+    return (
+        block[:, : 3 * width],
+        block[:, 3 * width : edge],
+        block[:, edge : edge + hidden],
+        block[:, edge + hidden :],
+    )
+
+
+def clip_forward(values, blocks, params):
+    (
+        gain_one,
+        shift_one,
+        qkv_bias,
+        proj_bias,
+        gain_two,
+        shift_two,
+        up_bias,
+        down_bias,
+    ) = params
+    centered_one, inv_one, normed_one = norm_forward(values, gain_one, shift_one)
+    qkv_parts, contexts, lses, pre_acts, activated = [], [], [], [], []
+    attended = proj_bias
+    for (qkv_full, proj_turned, up_full, down_turned), bias in zip(blocks, qkv_bias):
+        qkv = (contract(normed_one, qkv_full, 1, 0) + bias).astype(jnp.bfloat16)
+        context, lse = attention_forward(qkv)
+        attended = attended + contract(context, proj_turned, 1, 1)
+        qkv_parts.append(qkv)
+        contexts.append(context)
+        lses.append(lse)
+    hidden = values + attended
+    centered_two, inv_two, normed_two = norm_forward(hidden, gain_two, shift_two)
+    output = hidden + down_bias
+    for (qkv_full, proj_turned, up_full, down_turned), bias in zip(blocks, up_bias):
+        pre_act = contract(normed_two, up_full, 1, 0) + bias
+        active = exact_gelu(pre_act).astype(jnp.bfloat16)
+        output = output + contract(active, down_turned, 1, 1)
+        pre_acts.append(pre_act)
+        activated.append(active)
+    kept = (
+        centered_one,
+        inv_one,
+        normed_one,
+        qkv_parts,
+        contexts,
+        lses,
+        centered_two,
+        inv_two,
+        normed_two,
+        pre_acts,
+        activated,
+    )
+    return (output, kept)
+
+
+def clip_backward(grad_out, kept, blocks, params):
+    gain_one, gain_two = (params[0], params[4])
+    (
+        centered_one,
+        inv_one,
+        normed_one,
+        qkv_parts,
+        contexts,
+        lses,
+        centered_two,
+        inv_two,
+        normed_two,
+        pre_acts,
+        activated,
+    ) = kept
+    grad_down_bias = jnp.sum(grad_out, axis=0)
+    down_grad = grad_out.astype(jnp.bfloat16)
+    grad_normed_two = 0.0
+    up_biases, early, late, query_biases, value_biases = [], [], [], [], []
+    for (qkv_full, proj_turned, up_full, down_turned), pre_act, active in zip(
+        blocks, pre_acts, activated
+    ):
+        grad_down = contract(down_grad, active, 0, 0)
+        grad_act = contract(down_grad, down_turned, 1, 0)
+        grad_pre = jax.vjp(exact_gelu, pre_act)[1](grad_act)[0]
+        up_biases.append(jnp.sum(grad_pre, axis=0))
+        grad_pre_low = grad_pre.astype(jnp.bfloat16)
+        grad_up = contract(normed_two, grad_pre_low, 0, 0)
+        grad_normed_two = grad_normed_two + contract(grad_pre_low, up_full, 1, 1)
+        early.append((grad_up.astype(jnp.bfloat16), grad_down.astype(jnp.bfloat16)))
+    grad_hidden_norm, grad_gain_two, grad_shift_two = norm_backward(
+        grad_normed_two, centered_two, inv_two, gain_two
+    )
+    grad_hidden = grad_out + grad_hidden_norm
+    grad_proj_bias = jnp.sum(grad_hidden, axis=0)
+    proj_grad = grad_hidden.astype(jnp.bfloat16)
+    grad_normed_one = 0.0
+    for (qkv_full, proj_turned, up_full, down_turned), qkv, context, lse in zip(
+        blocks, qkv_parts, contexts, lses
+    ):
+        width = context.shape[1]
+        grad_proj = contract(proj_grad, context, 0, 0)
+        grad_context = contract(proj_grad, proj_turned, 1, 0).astype(jnp.bfloat16)
+        grad_qkv_low, bias_rows = attention_backward(qkv, grad_context, lse)
+        query_biases.append(bias_rows[0, :width])
+        value_biases.append(bias_rows[0, 2 * width :])
+        grad_qkv = contract(normed_one, grad_qkv_low, 0, 0)
+        grad_normed_one = grad_normed_one + contract(grad_qkv_low, qkv_full, 1, 1)
+        late.append((grad_qkv.astype(jnp.bfloat16), grad_proj.astype(jnp.bfloat16)))
+    grad_in_norm, grad_gain_one, grad_shift_one = norm_backward(
+        grad_normed_one, centered_one, inv_one, gain_one
+    )
+    grad_in = grad_hidden + grad_in_norm
+    whole = jnp.concatenate(
+        [
+            grad_gain_one,
+            grad_shift_one,
+            grad_proj_bias,
+            grad_gain_two,
+            grad_shift_two,
+            grad_down_bias,
+        ]
+    )
+    split = jnp.stack(
+        [jnp.concatenate(part) for part in zip(query_biases, value_biases, up_biases)]
+    )
+    return (grad_in, early, late, whole, split)
+
+
+GROUP = ("pipe", "col")
+EVERY = ("pipe", "col", "row")
+
+
+def trade(pieces, place, targets):
+    count = len(pieces)
+    stacked = jnp.stack(pieces)
+    taken = [lax.dynamic_index_in_dim(stacked, place, 0, keepdims=False)]
+    for step in range(1, count):
+        sent = lax.dynamic_index_in_dim(stacked, place ^ step, 0, keepdims=False)
+        taken.append(
+            lax.ppermute(
+                sent,
+                GROUP,
+                [(here, here ^ step) for here in range(count) if here ^ step in targets],
+            )
+        )
+    return taken
+
+
+def in_order(taken, place):
+    stacked = jnp.stack(taken)
+    return jnp.stack(
+        [
+            lax.dynamic_index_in_dim(stacked, place ^ index, 0, keepdims=False)
+            for index in range(len(taken))
+        ]
+    )
+
+
+def swap_columns(own, other, col):
+    got = lax.ppermute(other, "col", [(0, 1), (1, 0)])
+    return jnp.where(
+        col == 0, jnp.concatenate([own, got]), jnp.concatenate([got, own])
+    )
+
+
+def gather_blocks(block):
+    full = lax.all_gather(block, EVERY, axis=0, tiled=True)
+    return full.reshape(lax.axis_size(GROUP), -1, block.shape[1])
+
+
+def on_device_clip(
+    inputs,
+    first_gain,
+    first_shift,
+    qkv_weight,
+    query_bias,
+    value_bias,
+    proj_weight,
+    proj_bias,
+    second_gain,
+    second_shift,
+    up_weight,
+    up_bias,
+    down_weight,
+    down_bias,
+    cotangent,
+    live_clips,
+):
+    section, col = (lax.axis_index("pipe"), lax.axis_index("col"))
+    place = 2 * section + col
+    width, hidden_width = (qkv_weight.shape[3], up_weight.shape[2])
+    features = inputs.shape[3]
+    half = inputs.shape[2]
+    early_block = jnp.concatenate(
+        [qkv_weight[0, 0], qkv_weight[0, 1], qkv_weight[0, 2], proj_weight[0].T], axis=1
+    )
+    late_block = jnp.concatenate([up_weight[0], down_weight[0].T], axis=1)
+    early_full = gather_blocks(early_block)
+    late_full = gather_blocks(late_block)
+    vectors = lax.all_gather(
+        jnp.concatenate(
+            [
+                first_gain[0],
+                first_shift[0],
+                proj_bias[0],
+                second_gain[0],
+                second_shift[0],
+                down_bias[0],
+                query_bias[0],
+                value_bias[0],
+                up_bias[0],
+            ]
+        ),
+        GROUP,
+        axis=0,
+        tiled=False,
+    )
+    blocks, params = ([], [])
+    for layer in range(2):
+        blocks.append(
+            [
+                (
+                    early_full[2 * layer + part][:, : 3 * width],
+                    early_full[2 * layer + part][:, 3 * width :],
+                    late_full[2 * layer + part][:, :hidden_width],
+                    late_full[2 * layer + part][:, hidden_width:],
+                )
+                for part in range(2)
+            ]
+        )
+        rows = vectors[2 * layer]
+        whole = [rows[index * features : (index + 1) * features] for index in range(6)]
+        tails = [vectors[2 * layer + part][6 * features :] for part in range(2)]
+        params.append(
+            (
+                whole[0],
+                whole[1],
+                [
+                    jnp.concatenate(
+                        [tail[:width], jnp.zeros((width,), jnp.float32), tail[width : 2 * width]]
+                    )
+                    for tail in tails
+                ],
+                whole[2],
+                whole[3],
+                whole[4],
+                [tail[2 * width :] for tail in tails],
+                whole[5],
+            )
+        )
+
+    def own_clip(rows):
+        own = lax.dynamic_index_in_dim(rows[:, 0], place, 0, keepdims=False)
+        other = lax.dynamic_index_in_dim(rows[:, 0], place ^ 1, 0, keepdims=False)
+        return swap_columns(own, other, col)
+
+    values = own_clip(inputs).astype(jnp.float32)
+    live_flag = lax.dynamic_index_in_dim(live_clips[:, 0], place, 0, keepdims=False)
+    grad_final = own_clip(cotangent).astype(jnp.float32) * live_flag.astype(jnp.float32)
+    first, kept_first = clip_forward(values, blocks[0], params[0])
+    sent = first.astype(jnp.bfloat16)
+    second, kept_second = clip_forward(sent.astype(jnp.float32), blocks[1], params[1])
+    final = second.astype(jnp.bfloat16)
+    states = in_order(
+        trade([sent[:half], sent[half:], final[:half], final[half:]], place, (0, 1, 2, 3)), place
+    )
+
+    def reduce_grads(early, late):
+        quarter = hidden_width // 2
+        first_half = [
+            jnp.concatenate([part[0], part[1], up_part[0][:, :quarter]], axis=1)
+            for part, up_part in zip(late, early)
+        ]
+        second_half = [
+            jnp.concatenate([up_part[0][:, quarter:], up_part[1]], axis=1) for up_part in early
+        ]
+        stacked = jnp.concatenate(first_half + second_half, axis=0)
+        return lax.psum_scatter(stacked, EVERY, scatter_dimension=0, tiled=True)
+
+    grad_mid, early, late, whole_second, split_second = clip_backward(
+        grad_final, kept_second, blocks[1], params[1]
+    )
+    mid_low = grad_mid.astype(jnp.bfloat16)
+    own_second = reduce_grads(early, late)
+    mid_taken = trade([mid_low[:half], mid_low[half:]] * 2, place, (2, 3))
+    grad_start, early, late, whole_first, split_first = clip_backward(
+        mid_low.astype(jnp.float32), kept_first, blocks[0], params[0]
+    )
+    own_first = reduce_grads(early, late)
+    start_low = grad_start.astype(jnp.bfloat16)
+    start_taken = trade([start_low[:half], start_low[half:]] * 2, place, (0, 1))
+    grads_in = in_order(
+        [jnp.where(section == 1, mid, start) for mid, start in zip(mid_taken, start_taken)], place
+    ).astype(jnp.float32)
+    kept_half = jnp.where(section == 0, own_first, own_second)
+    moved = lax.ppermute(
+        jnp.where(section == 0, own_second, own_first), "pipe", [(0, 1), (1, 0)]
+    )
+    packed = jnp.where(
+        section == 0,
+        jnp.concatenate([kept_half, moved], axis=1),
+        jnp.concatenate([moved, kept_half], axis=1),
+    ).astype(jnp.float32)
+    grad_qkv, grad_proj, grad_up, grad_down = cut_block(packed, width, hidden_width)
+    whole_all, split_all = lax.psum(
+        (jnp.stack([whole_first, whole_second]), jnp.stack([split_first, split_second])), EVERY
+    )
+    whole_out = lax.dynamic_index_in_dim(whole_all, section, 0, keepdims=False).reshape(
+        6, 1, features
+    )
+    split_out = lax.dynamic_index_in_dim(split_all, section, 0, keepdims=False)
+    split_out = lax.dynamic_index_in_dim(split_out, col, 0, keepdims=False)
+    return (
+        states[None, :, None],
+        grads_in[None, :, None],
+        whole_out[0],
+        whole_out[1],
+        jnp.stack([grad_qkv[:, part * width : (part + 1) * width] for part in range(3)])[None],
+        split_out[None, :width],
+        split_out[None, width : 2 * width],
+        grad_proj.T[None],
+        whole_out[2],
+        whole_out[3],
+        whole_out[4],
+        grad_up[None],
+        split_out[None, 2 * width :],
+        grad_down.T[None],
+        whole_out[5],
+    )
+
+
+def one_clip_each(mesh):
+    sizes = dict(mesh.shape)
+    return sizes["pipe"] == 2 and sizes["col"] == 2
+
+
+def choose(mesh):
+    def body(*arrays):
+        fits = one_clip_each(mesh) and arrays[0].shape[:2] == (4, 1)
+        return (on_device_clip if fits else on_device)(*arrays)
+
+    return body
+
+
 def solution(mesh):
     placed = (
         P(None, "row", "col", None),
@@ -397,7 +876,7 @@
         P(None, "row"),
     )
     return jax.shard_map(
-        on_device,
+        choose(mesh),
         mesh=mesh,
         in_specs=placed,
         out_specs=(

time: 2840 us -> 618 us (0.22)
  waiting for transfers between devices: 1450 us -> 135 us
  matrix products: 729 us -> 145 us
  other arithmetic: 380 us -> 83.9 us
  Pallas kernels: 0 us -> 111 us
  local copies, waits for them, and re-layouts: 83.2 us -> 25.6 us
  loops' own time: 42.2 us -> 0 us
  blocking collectives: 109 us -> 72.2 us
    reduce_scatter x29 -> x2, waiting for transfers between devices: 762 us -> 28.6 us  [reduce_grads(): return lax.psum_scatter(stacked, EVERY, scatter_dimension=0, tiled=True)]
    dot_general x110 -> x48, matrix products: 729 us -> 145 us  [contract(): lax.dot_general(left, right, (((left_dim,), (right_dim,)), ((), ())), pre...]
    all_gather x32 -> x2, waiting for transfers between devices: 557 us -> 75.3 us  [gather_blocks(): full = lax.all_gather(block, EVERY, axis=0, tiled=True)]
    sub x10 -> x0, other arithmetic: 158 us -> none  [attention_probs(): return jax.nn.softmax(scores, axis=-1)]
    pallas_call x0 -> x8, Pallas kernels: none -> 111 us  [the longest x4 60.8 us: attention_backward(): pl.pallas_call(attention_backward_kernel, grid=(pairs,), in_specs=[column...]
    ppermute x10 -> x12, waiting for transfers between devices: 126 us -> 30.7 us  [the longest x9 30.1 us: trade(): lax.ppermute(sent, GROUP, [(here, here ^ step) for here in range(count) i...]
    concatenate x0 -> x9, other arithmetic: none -> 62.4 us  [the longest x2 59.3 us: reduce_grads(): stacked = jnp.concatenate(first_half + second_half, axis=0)]
    convert_element_type x16 -> x6, other arithmetic: 57.9 us -> 5.47 us  [the longest x1 3.57 us: on_device_clip(): grads_in = in_order([jnp.where(section == 1, mid, start) for mid, start i...]
  transfers between devices with their start and end apart: 71 -> 16, of which waited for: 68 -> 8; matrix products, arithmetic and copies ran while one was open for 7% -> 27% of each run, Pallas kernels for 0% -> 13%
where the time goes in v1:
time: 618 us; the launch traced here: 613 us
  matrix products  145 us (23%)
  waiting for transfers between devices  135 us (22%)
  Pallas kernels  111 us (18%)
  other arithmetic  83.9 us (14%)
  blocking collectives  72.2 us (12%)
  local copies, waits for them, and re-layouts  25.6 us (4%)
  starting transfers between devices  24.6 us (4%)
  between operations  16 us (3%)
    dot_general x48, matrix products, contract(): lax.dot_general(left, right, (((left_dim,), (right_dim,)), ((), ())), pre...  145 us
    all_gather x2, waiting for transfers between devices, gather_blocks(): full = lax.all_gather(block, EVERY, axis=0, tiled=True)  75.3 us
    pallas_call x4, Pallas kernels, attention_backward(): pl.pallas_call(attention_backward_kernel, grid=(pairs,), in_specs=[column...  60.8 us
    concatenate x2, other arithmetic, reduce_grads(): stacked = jnp.concatenate(first_half + second_half, axis=0)  59.3 us
    pallas_call x4, Pallas kernels, attention_forward(): pl.pallas_call(attention_forward_kernel, grid=(pairs,), in_specs=[column(...  50 us
    psum x1, blocking collectives, on_device_clip(): lax.psum((jnp.stack([whole_first, whole_second]), jnp.stack([split_first,...  46.8 us
    ppermute x9, waiting for transfers between devices, trade(): lax.ppermute(sent, GROUP, [(here, here ^ step) for here in range(count) i...  30.1 us
    reduce_scatter x2, waiting for transfers between devices, reduce_grads(): return lax.psum_scatter(stacked, EVERY, scatter_dimension=0, tiled=True)  28.6 us
  transfers between devices with their start and end apart: 16, of which 8 were waited for; matrix products, arithmetic and copies ran while one was open for 27% of the time, Pallas kernels for 13%

profile of v1, /device:TPU:0, one launch (start us, length us, event | category | flops | bytes accessed | tf_op | source)
XLA Modules:
  0.0 613.1 jit_solution(4471829497163923032)
XLA Ops:
  12.9 3.0 collective-permute-start
  18.7 25.4 %all-gather.1 = f32[4,1,4608]{2,1,0:T(1,128)S(1)} all-gather(f32[1,1,4608]{2,1,0:T(1,128)S(1)} %reshape.265), channel_id=2, replica_groups=mesh['pipe'=2,'row'=8,'col'=2] {'pipe','col'}, dimensions={0}, use_global_device_ids=true | all-gather | bytes 92160 | tf_op jit(solution)/shard_map/all_gather | solution.py:714
  47.2 29.7 %all-gather.5.cloned.1.call-done = bf16[2048,1024]{1,0:T(8,128)(2,1)} async-done(((bf16[64,1024]{1,0:T(8,128)(2,1)}), bf16[2048,1024]{1,0:T(8,128)(2,1)}) %all-gather.5.cloned.1.call-update) | async-done | bytes 4194320 | tf_op jit(solution)/shard_map/all_gather | solution.py:681
  76.9 2.3 add_convert_fusion.3.q_ref.k_ref.v_ref
  79.2 12.5 %attention_forward.4 = (bf16[1024,256]{1,0:T(8,128)(2,1)S(1)}, f32[2,8,1024]{2,1,0:T(8,128)S(1)}) custom-call(bf16[1024,768]{1,0:T(8,128)(2,1)S(1)} %add_convert_fusion.3.q_ref.k_ref.v_ref, bf16[1024,768]{1,0:T(8,128)(2,1)S(1)} %add_convert_fusion.3.q_ref.k_ref.v_ref, bf16[1024,768]{1,0:T(8,128)(2,1)S(1)} %add_convert_fusion.3.q_ref.k_ref.v_ref), custom_call_target="tpu_custom_call" | custom-call | flops 1073741824 | bytes 2097152 | tf_op jit(solution)/shard_map/attention_forward/pallas_call | solution.py:419
  91.8 2.4 add_convert_fusion.2.q_ref.k_ref.v_ref
  94.2 12.6 %attention_forward.5 = (bf16[1024,256]{1,0:T(8,128)(2,1)S(1)}, f32[2,8,1024]{2,1,0:T(8,128)S(1)}) custom-call(bf16[1024,768]{1,0:T(8,128)(2,1)S(1)} %add_convert_fusion.2.q_ref.k_ref.v_ref, bf16[1024,768]{1,0:T(8,128)(2,1)S(1)} %add_convert_fusion.2.q_ref.k_ref.v_ref, bf16[1024,768]{1,0:T(8,128)(2,1)S(1)} %add_convert_fusion.2.q_ref.k_ref.v_ref), custom_call_target="tpu_custom_call" | custom-call | flops 1073741824 | bytes 2097152 | tf_op jit(solution)/shard_map/attention_forward/pallas_call | solution.py:419
  110.8 45.5 %all-gather.7.cloned.1.call-done = bf16[2048,2048]{1,0:T(8,128)(2,1)} async-done(((bf16[64,2048]{1,0:T(8,128)(2,1)}), bf16[2048,2048]{1,0:T(8,128)(2,1)}) %all-gather.7.cloned.1.call-update) | async-done | bytes 8388624 | tf_op jit(solution)/shard_map/all_gather | solution.py:681
  156.3 13.2 %multiply_convert_fusion.3 = (bf16[1024,1024]{1,0:T(8,128)(2,1)S(1)}, f32[1024,1024]{1,0:T(8,128)}, f32[1024,1024]{1,0:T(8,128)}) fusion(f32[1024]{0:T(1024)S(1)} %bitcast.260, bf16[1024,512]{0,1:T(8,128)(2,1)S(1)} %add_convert_fusion.7, bf16[2048,2048]{1,0:T(8,128)(2,1)} %all-gather.7.cloned.1.call-done), kind=kOutput, calls=%fused_computation.53 | convolution fusion | flops 1142947840 | bytes 12587008 | tf_op jit(solution)/shard_map/dot_general | solution.py:383
  170.8 11.7 %multiply_convert_fusion.2 = (bf16[1024,1024]{1,0:T(8,128)(2,1)S(1)}, f32[1024,1024]{1,0:T(8,128)}, f32[1024,1024]{1,0:T(8,128)}) fusion(f32[1024]{0:T(1024)S(1)} %bitcast.258, bf16[1024,512]{0,1:T(8,128)(2,1)S(1)} %add_convert_fusion.7, bf16[2048,2048]{1,0:T(8,128)(2,1)S(1)} %copy-done.59), kind=kOutput, calls=%fused_computation.40 | convolution fusion | flops 1142947840 | bytes 12587008 | tf_op jit(solution)/shard_map/dot_general | solution.py:383
  187.1 12.4 %attention_forward.6 = (bf16[1024,256]{1,0:T(8,128)(2,1)S(1)}, f32[2,8,1024]{2,1,0:T(8,128)S(1)}) custom-call(bf16[1024,768]{1,0:T(8,128)(2,1)S(1)} %add_convert_fusion.1.q_ref.k_ref.v_ref, bf16[1024,768]{1,0:T(8,128)(2,1)S(1)} %add_convert_fusion.1.q_ref.k_ref.v_ref, bf16[1024,768]{1,0:T(8,128)(2,1)S(1)} %add_convert_fusion.1.q_ref.k_ref.v_ref), custom_call_target="tpu_custom_call" | custom-call | flops 1073741824 | bytes 2097152 | tf_op jit(solution)/shard_map/attention_forward/pallas_call | solution.py:419
  200.7 12.5 %attention_forward.7 = (bf16[1024,256]{1,0:T(8,128)(2,1)S(1)}, f32[2,8,1024]{2,1,0:T(8,128)S(1)}) custom-call(bf16[1024,768]{1,0:T(8,128)(2,1)S(1)} %add_convert_fusion.q_ref.k_ref.v_ref, bf16[1024,768]{1,0:T(8,128)(2,1)S(1)} %add_convert_fusion.q_ref.k_ref.v_ref, bf16[1024,768]{1,0:T(8,128)(2,1)S(1)} %add_convert_fusion.q_ref.k_ref.v_ref), custom_call_target="tpu_custom_call" | custom-call | flops 1073741824 | bytes 2097152 | tf_op jit(solution)/shard_map/attention_forward/pallas_call | solution.py:419
  215.0 26.7 %multiply_convert_fusion = (bf16[1024,1024]{1,0:T(8,128)(2,1)}, f32[1024,1024]{1,0:T(8,128)S(1)}, f32[1024,1024]{1,0:T(8,128)}) fusion(f32[1024]{0:T(1024)S(1)} %bitcast.264, bf16[1024,512]{0,1:T(8,128)(2,1)S(1)} %add_convert_fusion.5, bf16[2048,2048]{1,0:T(8,128)(2,1)S(1)} %copy-done.59), kind=kOutput, calls=%fused_computation.14 | convolution fusion | flops 1142947840 | bytes 12587008 | tf_op jit(solution)/shard_map/dot_general | solution.py:383
  241.7 6.3 %fusion.148 = (f32[1024]{0:T(1024)S(1)}, bf16[1024,1024]{1,0:T(8,128)(2,1)S(1)}) fusion(f32[1024,1024]{1,0:T(8,128)S(1)} %get-tuple-element.117, bf16[2048,2048]{1,0:T(8,128)(2,1)S(1)} %copy-done.59, f32[]{:T(128)} %bitcast.56, bf16[512,512]{0,1:T(8,128)(2,1)S(1)} %bitcast.206, bf16[512,512]{0,1:T(8,128)(2,1)} %collective-permute-done.4, pred[]{:T(512)S(6)} %eq.6, ...), kind=kOutput, calls=%fused_computation.344 | convolution fusion | flops 1096809472 | bytes 12591109 | tf_op jit(solution)/shard_map/dot_general | solution.py:383
  249.4 11.5 %multiply_convert_fusion.1 = (bf16[1024,1024]{1,0:T(8,128)(2,1)}, f32[1024,1024]{1,0:T(8,128)}, f32[1024,1024]{1,0:T(8,128)}) fusion(f32[1024]{0:T(1024)S(1)} %bitcast.262, bf16[1024,512]{0,1:T(8,128)(2,1)S(1)} %add_convert_fusion.5, bf16[2048,2048]{1,0:T(8,128)(2,1)S(1)} %copy-done.59), kind=kOutput, calls=%fused_computation.27 | convolution fusion | flops 1142947840 | bytes 12587008 | tf_op jit(solution)/shard_map/dot_general | solution.py:383
  260.9 7.4 %fusion.149 = (f32[1024]{0:T(1024)S(1)}, bf16[1024,1024]{1,0:T(8,128)(2,1)S(1)}) fusion(f32[1024,1024]{1,0:T(8,128)} %get-tuple-element.119, bf16[2048,2048]{1,0:T(8,128)(2,1)S(1)} %copy-done.59, f32[]{:T(128)} %bitcast.56, bf16[512,512]{0,1:T(8,128)(2,1)S(1)} %bitcast.207, bf16[512,512]{0,1:T(8,128)(2,1)} %collective-permute-done.4, pred[]{:T(512)S(6)} %eq.6, ...), kind=kOutput, calls=%fused_computation.345 | convolution fusion | flops 1096809472 | bytes 12591109 | tf_op jit(solution)/shard_map/dot_general | solution.py:383
  270.9 2.0 multiply_reduce_fusion
  272.9 3.2 fusion.128
  277.6 15.2 %attention_backward.4 = (bf16[1024,768]{1,0:T(8,128)(2,1)S(1)}, f32[8,768]{1,0:T(8,128)S(1)}) custom-call(bf16[1024,768]{1,0:T(8,128)(2,1)S(1)} %add_convert_fusion.1.q_ref.k_ref.v_ref, bf16[1024,768]{1,0:T(8,128)(2,1)S(1)} %add_convert_fusion.1.q_ref.k_ref.v_ref, bf16[1024,768]{1,0:T(8,128)(2,1)S(1)} %add_convert_fusion.1.q_ref.k_ref.v_ref, ...), custom_call_target="tpu_custom_call" | custom-call | flops 2684354560 | bytes 3670016 | tf_op jit(solution)/shard_map/attention_backward/pallas_call | solution.py:490
  294.5 15.0 %attention_backward.5 = (bf16[1024,768]{1,0:T(8,128)(2,1)S(1)}, f32[8,768]{1,0:T(8,128)S(1)}) custom-call(bf16[1024,768]{1,0:T(8,128)(2,1)S(1)} %add_convert_fusion.q_ref.k_ref.v_ref, bf16[1024,768]{1,0:T(8,128)(2,1)S(1)} %add_convert_fusion.q_ref.k_ref.v_ref, bf16[1024,768]{1,0:T(8,128)(2,1)S(1)} %add_convert_fusion.q_ref.k_ref.v_ref, ...), custom_call_target="tpu_custom_call" | custom-call | flops 2684354560 | bytes 3670016 | tf_op jit(solution)/shard_map/attention_backward/pallas_call | solution.py:490
  311.1 3.3 convolution_convert_fusion
  314.4 3.1 convolution_convert_fusion.1
  317.5 29.7 %maximum_maximum_fusion.1 = bf16[2048,1536]{1,0:T(8,128)(2,1)} fusion(bf16[512,1024]{1,0:T(8,128)(2,1)S(1)} %convolution_convert_fusion, bf16[512,512]{1,0:T(8,128)(2,1)S(1)} %get-tuple-element.243, bf16[512,1024]{1,0:T(8,128)(2,1)S(1)} %convolution_convert_fusion.1, bf16[512,512]{1,0:T(8,128)(2,1)S(1)} %get-tuple-element.152, ...), kind=kLoop, calls=%fused_computation.1 | loop fusion | flops 62914560 | bytes 12582912 | tf_op jit(solution)/shard_map/concatenate | solution.py:791
  347.3 2.3 fusion.90
  349.6 2.9 fusion.43
  355.7 3.2 fusion.151
  362.7 3.1 fusion.150
  365.8 1.9 multiply_reduce_fusion.1
  368.8 2.3 convolution_convert_fusion.13.grad_ref
  371.2 15.3 %attention_backward.6 = (bf16[1024,768]{1,0:T(8,128)(2,1)S(1)}, f32[8,768]{1,0:T(8,128)S(1)}) custom-call(bf16[1024,768]{1,0:T(8,128)(2,1)S(1)} %copy-done.7, bf16[1024,768]{1,0:T(8,128)(2,1)S(1)} %copy-done.7, bf16[1024,768]{1,0:T(8,128)(2,1)S(1)} %copy-done.7, bf16[1024,256]{1,0:T(8,128)(2,1)S(1)} %convolution_convert_fusion.13.grad_ref, ...), custom_call_target="tpu_custom_call" | custom-call | flops 2684354560 | bytes 3670016 | tf_op jit(solution)/shard_map/attention_backward/pallas_call | solution.py:490
  388.0 15.2 %attention_backward.7 = (bf16[1024,768]{1,0:T(8,128)(2,1)S(1)}, f32[8,768]{1,0:T(8,128)S(1)}) custom-call(bf16[1024,768]{1,0:T(8,128)(2,1)S(1)} %copy-done.5, bf16[1024,768]{1,0:T(8,128)(2,1)S(1)} %copy-done.5, bf16[1024,768]{1,0:T(8,128)(2,1)S(1)} %copy-done.5, bf16[1024,256]{1,0:T(8,128)(2,1)S(1)} %convolution_convert_fusion.12.grad_ref, ...), custom_call_target="tpu_custom_call" | custom-call | flops 2684354560 | bytes 3670016 | tf_op jit(solution)/shard_map/attention_backward/pallas_call | solution.py:490
  413.7 29.6 %maximum_maximum_fusion = bf16[2048,1536]{1,0:T(8,128)(2,1)} fusion(bf16[512,1024]{1,0:T(8,128)(2,1)S(1)} %convolution_convert_fusion.4, bf16[512,512]{1,0:T(8,128)(2,1)S(1)} %get-tuple-element.150, bf16[512,1024]{1,0:T(8,128)(2,1)S(1)} %convolution_convert_fusion.5, bf16[512,512]{1,0:T(8,128)(2,1)S(1)} %get-tuple-element.148, ...), kind=kLoop, calls=%fused_computation | loop fusion | flops 62914560 | bytes 12582912 | tf_op jit(solution)/shard_map/concatenate | solution.py:791
  443.4 2.3 fusion.95
  446.1 3.1 fusion.52
  453.4 3.3 collective-permute-start.6
  456.8 3.2 collective-permute-start.7
  461.5 46.8 %all-reduce = (f32[2,3072]{1,0:T(2,128)S(1)}, f32[2,2,1536]{2,1,0:T(2,128)S(1)}) all-reduce(f32[2,3072]{1,0:T(2,128)S(1)} %pad_maximum_fusion.7, f32[2,2,1536]{2,1,0:T(2,128)S(1)} %pad_maximum_fusion.8), channel_id=1, replica_groups=mesh['pipe'=2,'row'=8,'col'=2] {'pipe','col','row'}, use_global_device_ids=true, to_apply=%region_28.29 | all-reduce | flops 12288 | bytes 98304 | tf_op jit(solution)/shard_map/psum | solution.py:819
  509.1 3.3 fusion.72
  512.4 2.5 add_convert_fusion.4
  519.3 5.5 collective-permute-start.9
  524.8 2.3 collective-permute-start.1
  530.9 11.2 %collective-permute-done.10 = bf16[512,512]{0,1:T(8,128)(2,1)S(1)} collective-permute-done((bf16[512,512]{0,1:T(8,128)(2,1)S(1)}, bf16[512,512]{0,1:T(8,128)(2,1)S(1)}, u32[]{:S(2)}, u32[]{:S(2)}) %collective-permute-start.10) | collective-permute-done | bytes 524320 | tf_op jit(solution)/shard_map/ppermute | solution.py:654
  545.1 6.8 %collective-permute-done.1 = bf16[512,512]{0,1:T(8,128)(2,1)} collective-permute-done((bf16[512,512]{0,1:T(8,128)(2,1)}, bf16[512,512]{0,1:T(8,128)(2,1)}, u32[]{:S(2)}, u32[]{:S(2)}) %collective-permute-start.1) | collective-permute-done | bytes 524320 | tf_op jit(solution)/shard_map/ppermute | solution.py:654
  552.8 11.2 %collective-permute-done.3 = bf16[512,512]{0,1:T(8,128)(2,1)} collective-permute-done((bf16[512,512]{0,1:T(8,128)(2,1)}, bf16[512,512]{0,1:T(8,128)(2,1)}, u32[]{:S(2)}, u32[]{:S(2)}) %collective-permute-start.3) | collective-permute-done | bytes 524320 | tf_op jit(solution)/shard_map/ppermute | solution.py:654
  564.0 1.8 pad_maximum_fusion.1
  566.2 2.4 copy.101
  568.6 28.6 %reduce-scatter.3.cloned.1.call-done = bf16[64,1536]{1,0:T(8,128)(2,1)} async-done(((bf16[2048,1536]{1,0:T(8,128)(2,1)}), bf16[64,1536]{1,0:T(8,128)(2,1)}) %reduce-scatter.3.cloned.1.call-update) | async-done | bytes 196624 | tf_op jit(solution)/shard_map/reduce_scatter | solution.py:792
  599.8 3.6 maximum_convert_fusion
  (316 shorter events, 76.6 us)
Async XLA Ops:
  7.2 69.7 %all-gather.5.cloned.1.call-start = ((), (), s32[]{:S(2)}) async-start(), calls=%async_computation.2 | async-start | bytes 4325376 | tf_op jit(solution)/shard_map/all_gather | solution.py:681
  9.5 9.1 %copy-start.53 = (f32[1,512]{1,0:T(1,128)S(1)}, f32[1,512]{1,0:T(1,128)}, u32[]{:S(2)}) copy-start(f32[1,512]{1,0:T(1,128)} %param.23) | copy-start | bytes 6148
  9.5 9.1 %copy-start.54 = (f32[1,512]{1,0:T(1,128)S(1)}, f32[1,512]{1,0:T(1,128)}, u32[]{:S(2)}) copy-start(f32[1,512]{1,0:T(1,128)} %param.24) | copy-start | bytes 6148
  9.5 9.1 %copy-start.55 = (f32[1,512]{1,0:T(1,128)S(1)}, f32[1,512]{1,0:T(1,128)}, u32[]{:S(2)}) copy-start(f32[1,512]{1,0:T(1,128)} %param.25) | copy-start | bytes 6148
  9.5 9.1 %copy-start.56 = (f32[1,512]{1,0:T(1,128)S(1)}, f32[1,512]{1,0:T(1,128)}, u32[]{:S(2)}) copy-start(f32[1,512]{1,0:T(1,128)} %param.29) | copy-start | bytes 6148
  9.5 9.1 %copy-start.57 = (f32[1,256]{1,0:T(1,128)S(1)}, f32[1,256]{1,0:T(1,128)}, u32[]{:S(2)}) copy-start(f32[1,256]{1,0:T(1,128)} %param.20) | copy-start | bytes 3076
  9.5 9.1 %copy-start.58 = (f32[1,256]{1,0:T(1,128)S(1)}, f32[1,256]{1,0:T(1,128)}, u32[]{:S(2)}) copy-start(f32[1,256]{1,0:T(1,128)} %param.21) | copy-start | bytes 3076
  9.5 9.1 %copy-start.45 = (f32[1,1024]{1,0:T(1,128)S(1)}, f32[1,1024]{1,0:T(1,128)}, u32[]{:S(2)}) copy-start(f32[1,1024]{1,0:T(1,128)} %param.27) | copy-start | bytes 12292
  9.5 146.8 %all-gather.7.cloned.1.call-start = ((), (), s32[]{:S(2)}) async-start(), calls=%async_computation.3 | async-start | bytes 8650752 | tf_op jit(solution)/shard_map/all_gather | solution.py:681
  11.3 557.3 %reduce-scatter.5.cloned.1.call-start = ((), (), s32[]{:S(2)}) async-start(), calls=%async_computation.5 | async-start | bytes 6488064 | tf_op jit(solution)/shard_map/reduce_scatter | solution.py:792
  11.4 33.7 %copy-start.60 = (s32[4,1]{0,1:T(1,128)S(1)}, s32[4,1]{0,1:T(1,128)}, u32[]{:S(2)}) copy-start(s32[4,1]{0,1:T(1,128)} %param.31) | copy-start | bytes 52
  12.9 33.5 %collective-permute-start = (bf16[512,512]{0,1:T(8,128)(2,1)S(1)}, bf16[512,512]{0,1:T(8,128)(2,1)S(1)}, u32[]{:S(2)}, u32[]{:S(2)}) collective-permute-start(bf16[512,512]{0,1:T(8,128)(2,1)S(1)} %bitcast.211), channel_id=1, source_target_pairs={{0,1},{1,0},{2,3},{3,2},{4,5},{5,4},{6,7},{7,6},{8,9},{9,8},{10,11... | collective-permute-start | bytes 1572872 | tf_op jit(solution)/shard_map/ppermute | solution.py:674
  18.2 223.5 %collective-permute-start.4 = (bf16[512,512]{0,1:T(8,128)(2,1)}, bf16[512,512]{0,1:T(8,128)(2,1)}, u32[]{:S(2)}, u32[]{:S(2)}) collective-permute-start(bf16[512,512]{0,1:T(8,128)(2,1)} %bitcast.55), channel_id=1, source_target_pairs={{0,1},{1,0},{2,3},{3,2},{4,5},{5,4},{6,7},{7,6},{8,9},{9,8},{10,11... | collective-permute-start | bytes 1572872 | tf_op jit(solution)/shard_map/ppermute | solution.py:674
  18.5 90.0 %copy-start.19 = (bf16[1,1,512,512]{2,3,1,0:T(8,128)(2,1)}, bf16[1,1,512,512]{2,3,1,0:T(8,128)(2,1)S(1)}, u32[]{:S(2)}) copy-start(bf16[1,1,512,512]{2,3,1,0:T(8,128)(2,1)S(1)} %copy.77) | copy-start | bytes 1572868
  46.3 45.4 %copy-start.43 = (f32[1,512]{1,0:T(1,128)}, f32[1,512]{1,0:T(1,128)S(1)}, u32[]{:S(2)}) copy-start(f32[1,512]{1,0:T(1,128)S(1)} %get-tuple-element.185) | copy-start | bytes 6148
  46.3 45.4 %copy-start.49 = (f32[1,512]{1,0:T(1,128)}, f32[1,512]{1,0:T(1,128)S(1)}, u32[]{:S(2)}) copy-start(f32[1,512]{1,0:T(1,128)S(1)} %get-tuple-element.184) | copy-start | bytes 6148
  46.3 64.1 %copy-start.37 = (f32[1,512]{1,0:T(1,128)}, f32[1,512]{1,0:T(1,128)S(1)}, u32[]{:S(2)}) copy-start(f32[1,512]{1,0:T(1,128)S(1)} %get-tuple-element.182) | copy-start | bytes 6148
  46.3 110.0 %copy-start.46 = (f32[1,1024]{1,0:T(1,128)}, f32[1,1024]{1,0:T(1,128)S(1)}, u32[]{:S(2)}) copy-start(f32[1,1024]{1,0:T(1,128)S(1)} %get-tuple-element.190) | copy-start | bytes 12292
  46.4 62.1 %copy-start.22 = (bf16[512,512]{0,1:T(8,128)(2,1)}, bf16[512,512]{0,1:T(8,128)(2,1)S(1)}, u32[]{:S(2)}) copy-start(bf16[512,512]{0,1:T(8,128)(2,1)S(1)} %collective-permute-done) | copy-start | bytes 1572868
  46.7 45.1 %copy-start.33 = (f32[1024]{0:T(1024)}, f32[1024]{0:T(1024)S(1)}, u32[]{:S(2)}) copy-start(f32[1024]{0:T(1024)S(1)} %broadcast_multiply_fusion.11) | copy-start | bytes 12292
  47.1 44.6 %copy-start.39 = (f32[1024]{0:T(1024)}, f32[1024]{0:T(1024)S(1)}, u32[]{:S(2)}) copy-start(f32[1024]{0:T(1024)S(1)} %add_rsqrt_fusion.3) | copy-start | bytes 12292
  79.2 12.6 %copy-start.6 = (bf16[1024,768]{1,0:T(8,128)(2,1)}, bf16[1024,768]{1,0:T(8,128)(2,1)S(1)}, u32[]{:S(2)}) copy-start(bf16[1024,768]{1,0:T(8,128)(2,1)S(1)} %add_convert_fusion.3.q_ref.k_ref.v_ref) | copy-start | bytes 4718596
  91.7 15.1 %copy-start = (bf16[1024,256]{1,0:T(8,128)(2,1)}, bf16[1024,256]{1,0:T(8,128)(2,1)S(1)}, u32[]{:S(2)}) copy-start(bf16[1024,256]{1,0:T(8,128)(2,1)S(1)} %get-tuple-element.31) | copy-start | bytes 1572868
  94.2 14.2 %copy-start.4 = (bf16[1024,768]{1,0:T(8,128)(2,1)}, bf16[1024,768]{1,0:T(8,128)(2,1)S(1)}, u32[]{:S(2)}) copy-start(bf16[1024,768]{1,0:T(8,128)(2,1)S(1)} %add_convert_fusion.2.q_ref.k_ref.v_ref) | copy-start | bytes 4718596
  110.1 72.5 %copy-start.10 = (f32[1024,512]{0,1:T(8,128)}, f32[1024,512]{0,1:T(8,128)S(1)}, u32[]{:S(2)}) copy-start(f32[1024,512]{0,1:T(8,128)S(1)} %get-tuple-element.220) | copy-start | bytes 6291460
  110.1 59.4 %copy-start.31 = (f32[1024]{0:T(1024)}, f32[1024]{0:T(1024)S(1)}, u32[]{:S(2)}) copy-start(f32[1024]{0:T(1024)S(1)} %broadcast_multiply_fusion.10) | copy-start | bytes 12292
  110.4 59.1 %copy-start.35 = (f32[1024]{0:T(1024)}, f32[1024]{0:T(1024)S(1)}, u32[]{:S(2)}) copy-start(f32[1024]{0:T(1024)S(1)} %add_rsqrt_fusion.2) | copy-start | bytes 12292
  110.8 60.0 %copy-start.28 = (bf16[1024,512]{0,1:T(8,128)(2,1)}, bf16[1024,512]{0,1:T(8,128)(2,1)S(1)}, u32[]{:S(2)}) copy-start(bf16[1024,512]{0,1:T(8,128)(2,1)S(1)} %add_convert_fusion.7) | copy-start | bytes 3145732
  156.3 13.2 %copy-start.59 = (bf16[2048,2048]{1,0:T(8,128)(2,1)S(1)}, bf16[2048,2048]{1,0:T(8,128)(2,1)}, u32[]{:S(2)}) copy-start(bf16[2048,2048]{1,0:T(8,128)(2,1)} %all-gather.7.cloned.1.call-done) | copy-start | bytes 25165828
  183.9 125.5 %copy-start.16 = (bf16[1024,512]{0,1:T(8,128)(2,1)}, bf16[1024,512]{0,1:T(8,128)(2,1)S(1)}, u32[]{:S(2)}) copy-start(bf16[1024,512]{0,1:T(8,128)(2,1)S(1)} %get-tuple-element.224) | copy-start | bytes 3145732
  214.4 58.5 %copy-start.8 = (f32[1024,512]{0,1:T(8,128)}, f32[1024,512]{0,1:T(8,128)S(1)}, u32[]{:S(2)}) copy-start(f32[1024,512]{0,1:T(8,128)S(1)} %get-tuple-element.226) | copy-start | bytes 6291460
  215.0 26.7 %copy-start.27 = (bf16[1,1,512,512]{2,3,1,0:T(8,128)(2,1)S(1)}, bf16[1,1,512,512]{2,3,1,0:T(8,128)(2,1)}, u32[]{:S(2)}) copy-start(bf16[1,1,512,512]{2,3,1,0:T(8,128)(2,1)} %copy.83) | copy-start | bytes 1572868
  347.2 250.0 %reduce-scatter.3.cloned.1.call-start = ((), (), s32[]{:S(2)}) async-start(), calls=%async_computation.4 | async-start | bytes 6488064 | tf_op jit(solution)/shard_map/reduce_scatter | solution.py:792
  371.2 16.8 %copy-start.5 = (bf16[1024,768]{1,0:T(8,128)(2,1)S(1)}, bf16[1024,768]{1,0:T(8,128)(2,1)}, u32[]{:S(2)}) copy-start(bf16[1024,768]{1,0:T(8,128)(2,1)} %copy-done.4) | copy-start | bytes 4718596
  388.0 16.3 %copy-start.29 = (bf16[1024,512]{0,1:T(8,128)(2,1)S(1)}, bf16[1024,512]{0,1:T(8,128)(2,1)}, u32[]{:S(2)}) copy-start(bf16[1024,512]{0,1:T(8,128)(2,1)} %copy-done.28) | copy-start | bytes 3145732
  450.6 10.6 %copy-start.42 = (f32[3072]{0:T(1024)S(1)}, f32[3072]{0:T(1024)}, u32[]{:S(2)}) copy-start(f32[3072]{0:T(1024)} %custom-call.1) | copy-start | bytes 36868
  450.6 10.7 %copy-start.41 = (f32[3072]{0:T(1024)S(1)}, f32[3072]{0:T(1024)}, u32[]{:S(2)}) copy-start(f32[3072]{0:T(1024)} %custom-call) | copy-start | bytes 36868
  450.6 58.4 %copy-start.18 = (bf16[1024,512]{0,1:T(8,128)(2,1)S(1)}, bf16[1024,512]{0,1:T(8,128)(2,1)}, u32[]{:S(2)}) copy-start(bf16[1024,512]{0,1:T(8,128)(2,1)} %copy-done.16) | copy-start | bytes 3145732
  452.0 67.4 %collective-permute-start.5 = (bf16[512,512]{0,1:T(8,128)(2,1)}, bf16[512,512]{0,1:T(8,128)(2,1)}, u32[]{:S(2)}, u32[]{:S(2)}) collective-permute-start(bf16[512,512]{0,1:T(8,128)(2,1)} %get-tuple-element.131), channel_id=1, source_target_pairs={{16,17},{17,16},{18,19},{19,18},{20,21},{21,20},{22,23},{23,22},{2... | collective-permute-start | bytes 1572872 | tf_op jit(solution)/shard_map/ppermute | solution.py:654
  453.4 71.4 %collective-permute-start.6 = (bf16[512,512]{0,1:T(8,128)(2,1)}, bf16[512,512]{0,1:T(8,128)(2,1)}, u32[]{:S(2)}, u32[]{:S(2)}) collective-permute-start(bf16[512,512]{0,1:T(8,128)(2,1)} %get-tuple-element.134), channel_id=1, source_target_pairs={{0,1},{1,0},{2,3},{3,2},{4,5},{5,4},{6,7},{7,6},{8,9},{9,8},{10,11... | collective-permute-start | bytes 1572872 | tf_op jit(solution)/shard_map/ppermute | solution.py:654
  456.8 71.5 %collective-permute-start.7 = (bf16[512,512]{0,1:T(8,128)(2,1)}, bf16[512,512]{0,1:T(8,128)(2,1)}, u32[]{:S(2)}, u32[]{:S(2)}) collective-permute-start(bf16[512,512]{0,1:T(8,128)(2,1)} %get-tuple-element.130), channel_id=1, source_target_pairs={{0,16},{1,17},{2,18},{3,19},{4,20},{5,21},{6,22},{7,23},{8,24},{9,... | collective-permute-start | bytes 1572872 | tf_op jit(solution)/shard_map/ppermute | solution.py:654
  459.9 68.4 %collective-permute-start.8 = (bf16[512,512]{0,1:T(8,128)(2,1)S(1)}, bf16[512,512]{0,1:T(8,128)(2,1)}, u32[]{:S(2)}, u32[]{:S(2)}) collective-permute-start(bf16[512,512]{0,1:T(8,128)(2,1)S(1)} %get-tuple-element.133), channel_id=1, source_target_pairs={{16,0},{17,1},{18,2},{19,3},{20,4},{21,5},{22,6},{23,7},{24,8},{25... | collective-permute-start | bytes 1572872 | tf_op jit(solution)/shard_map/ppermute | solution.py:654
  516.0 26.2 %collective-permute-start.10 = (bf16[512,512]{0,1:T(8,128)(2,1)S(1)}, bf16[512,512]{0,1:T(8,128)(2,1)S(1)}, u32[]{:S(2)}, u32[]{:S(2)}) collective-permute-start(bf16[512,512]{0,1:T(8,128)(2,1)S(1)} %get-tuple-element.132), channel_id=1, source_target_pairs={{16,1},{17,0},{18,3},{19,2},{20,5},{21,4},{22,7},{23,6},{24,9},{25... | collective-permute-start | bytes 1572872 | tf_op jit(solution)/shard_map/ppermute | solution.py:654
  519.3 22.8 %collective-permute-start.9 = (bf16[512,512]{0,1:T(8,128)(2,1)S(1)}, bf16[512,512]{0,1:T(8,128)(2,1)S(1)}, u32[]{:S(2)}, u32[]{:S(2)}) collective-permute-start(bf16[512,512]{0,1:T(8,128)(2,1)S(1)} %get-tuple-element.129), channel_id=1, source_target_pairs={{0,17},{1,16},{2,19},{3,18},{4,21},{5,20},{6,23},{7,22},{8,25},{9,... | collective-permute-start | bytes 1572872 | tf_op jit(solution)/shard_map/ppermute | solution.py:654
  524.8 27.1 %collective-permute-start.1 = (bf16[512,512]{0,1:T(8,128)(2,1)}, bf16[512,512]{0,1:T(8,128)(2,1)}, u32[]{:S(2)}, u32[]{:S(2)}) collective-permute-start(bf16[512,512]{0,1:T(8,128)(2,1)} %get-tuple-element.144), channel_id=1, source_target_pairs={{0,1},{1,0},{16,17},{17,16},{2,3},{3,2},{18,19},{19,18},{4,5},{5,4... | collective-permute-start | bytes 1572872 | tf_op jit(solution)/shard_map/ppermute | solution.py:654
  528.3 24.5 %collective-permute-start.2 = (bf16[512,512]{0,1:T(8,128)(2,1)}, bf16[512,512]{0,1:T(8,128)(2,1)}, u32[]{:S(2)}, u32[]{:S(2)}) collective-permute-start(bf16[512,512]{0,1:T(8,128)(2,1)} %get-tuple-element.143), channel_id=1, source_target_pairs={{0,16},{1,17},{16,0},{17,1},{2,18},{3,19},{18,2},{19,3},{4,20},{5,... | collective-permute-start | bytes 1572872 | tf_op jit(solution)/shard_map/ppermute | solution.py:654
  528.4 35.6 %collective-permute-start.3 = (bf16[512,512]{0,1:T(8,128)(2,1)}, bf16[512,512]{0,1:T(8,128)(2,1)}, u32[]{:S(2)}, u32[]{:S(2)}) collective-permute-start(bf16[512,512]{0,1:T(8,128)(2,1)} %get-tuple-element.142), channel_id=1, source_target_pairs={{0,17},{1,16},{16,1},{17,0},{2,19},{3,18},{18,3},{19,2},{4,21},{5,... | collective-permute-start | bytes 1572872 | tf_op jit(solution)/shard_map/ppermute | solution.py:654
  598.2 5.7 collective-permute-start.11
  (42 other events, 120.7 us)
Sparse Core Ops, SparseCore 0:
  11.6 65.2 all-gather.4
  80.4 75.8 all-gather.6
  347.3 113.1 reduce-scatter.4
  466.9 130.2 reduce-scatter.2
